TPU v7x, 32 devices: a whole 2x2x4 slice. The times are simulated.
32 devices in a mesh: cube: 4 (over y, x), grid: 8 (over z, core).
Axes of the slice: x: 2, y: 2, z: 4, core: 2. Of those that a mesh axis runs over, the one named last changes fastest.
Arguments:
- parent_front: float32 [8192, 4, 4096], P('grid', 'cube'), as said below
- child_block: bfloat16 [4, 6144, 6144], P('cube', 'grid'), as said below
- child_panel: bfloat16 [4, 6144, 512], P('cube', 'grid'), may hold values from -0.15625 to 0.15625
- row_map: int32 [4, 6144], replicated, may hold values from 0 to 8191, as said below
Outputs:
- schur_block: float32 [8192, 4, 4096], P('grid', 'cube')
- panel_factor: float32 [8192, 4, 256], P('grid', 'cube')
Inputs may be any that keep to these rules, and one draw needn't show every extreme that they name: Each row of row_map lists 6144 distinct parent rows. Cut the 6144 entries of a row into 768 entries for each grid index, and the parent rows into blocks of 1024: from one grid index at most 192 entries fall into one block, a number reached in every draw. `parent_front`: symmetric with a dominant positive diagonal. `child_block`: symmetric with a dominant positive diagonal.
All inputs are finite; a program needn't handle non-finite values.
Results may differ from a plain program's by a relative error of at most 0.0015.
Values may be sent and summed in bfloat16 or wider, within the bound.
A program may use at most 192 MiB of HBM per device.

v0:
```python
import jax
import jax.numpy as jnp
from jax import lax
from jax.sharding import PartitionSpec as P

PW = 512


def swapped(block, axis, distance):
    count = lax.axis_size(axis)
    route = []
    for low in range(count):
        high = low | 1 << distance
        if high != low and high < count:
            route += [(low, high), (high, low)]
    return lax.ppermute(block, axis, route)


def spread_columns(contrib_rows, column_map, front_order):
    block_width = min(512, front_order)

    def place_block(block_number, buffer_cols):
        targets = block_number * block_width + lax.iota(jnp.int32, block_width)
        one_hot = (column_map[:, None] == targets[None, :]).astype(jnp.bfloat16)
        placed_part = jnp.dot(contrib_rows, one_hot, preferred_element_type=jnp.float32).astype(
            jnp.bfloat16
        )
        return lax.dynamic_update_slice_in_dim(
            buffer_cols, placed_part, block_number * block_width, 1
        )

    initial = jnp.zeros((contrib_rows.shape[0], front_order), jnp.bfloat16)
    return lax.fori_loop(0, front_order // block_width, place_block, initial)


def parity_columns(matrix, parity):
    paired = matrix.reshape(matrix.shape[0], matrix.shape[1] // 2, 2)
    return lax.dynamic_index_in_dim(paired, parity, 2, keepdims=False)


def pack_rows(slab_rows, local_map, owned_rows, owners, capacity):
    owner_of = local_map // owned_rows
    owner_hot = (owner_of[:, None] == lax.iota(jnp.int32, owners)[None, :]).astype(jnp.int32)
    rank_of = jnp.sum((jnp.cumsum(owner_hot, axis=0) - 1) * owner_hot, axis=1)
    slot_of = owner_of * capacity + rank_of
    selector = (lax.iota(jnp.int32, owners * capacity)[:, None] == slot_of[None, :]).astype(
        jnp.bfloat16
    )
    packed = jnp.dot(selector, slab_rows, preferred_element_type=jnp.float32).astype(jnp.bfloat16)
    return packed.reshape(owners, capacity, slab_rows.shape[1])


def placement_matrix(full_map, grid_pos, owned_rows, owners, capacity):
    mine_mask = full_map // owned_rows == grid_pos
    by_source = mine_mask.reshape(owners, -1).astype(jnp.int32)
    rank_of = jnp.cumsum(by_source, axis=1) - 1
    column_of = (lax.iota(jnp.int32, owners)[:, None] * capacity + rank_of).reshape(-1)
    local_row = full_map - grid_pos * owned_rows
    row_hot = (
        (local_row[:, None] == lax.iota(jnp.int32, owned_rows)[None, :]) & mine_mask[:, None]
    ).astype(jnp.bfloat16)
    column_hot = (column_of[:, None] == lax.iota(jnp.int32, owners * capacity)[None, :]).astype(
        jnp.bfloat16
    )
    return jnp.einsum("ir,iq->rq", row_hot, column_hot, preferred_element_type=jnp.float32).astype(
        jnp.bfloat16
    )


def place_rows(received, matrix):
    flat_rows = received.reshape(-1, received.shape[2])
    return jnp.dot(matrix, flat_rows, preferred_element_type=jnp.float32)


def shards(parent_front, child_block, child_panel, row_map):
    owners = lax.axis_size("grid")
    cube_pos = lax.axis_index("cube")
    grid_pos = lax.axis_index("grid")
    half_index = cube_pos % 2
    other_index = 1 - half_index
    partner_pos = jnp.bitwise_xor(cube_pos, 1)
    child_rows = child_block.shape[1]
    owned_rows = parent_front.shape[0]
    half_cols = parent_front.shape[2]
    front_order = 2 * half_cols
    capacity = 2 * child_rows // owners
    own_panel = child_panel[0]
    products = jnp.einsum(
        "ik,jk->ij",
        own_panel,
        lax.all_gather(child_panel, "grid", axis=1, tiled=True)[0],
        preferred_element_type=jnp.float32,
    )
    contrib_rows = (child_block[0].astype(jnp.float32) - products).astype(jnp.bfloat16)
    own_map = lax.dynamic_index_in_dim(row_map, cube_pos, 0, keepdims=False)
    partner_map = lax.dynamic_index_in_dim(row_map, partner_pos, 0, keepdims=False)
    own_local = lax.dynamic_slice_in_dim(own_map, grid_pos * child_rows, child_rows)
    partner_local = lax.dynamic_slice_in_dim(partner_map, grid_pos * child_rows, child_rows)
    spread = spread_columns(contrib_rows, own_map, front_order)
    own_half = parity_columns(spread, half_index)
    other_half = parity_columns(spread, other_index)
    partner_half = swapped(other_half, "cube", 0)
    sent_own = pack_rows(own_half, own_local, owned_rows, owners, capacity)
    sent_partner = pack_rows(partner_half, partner_local, owned_rows, owners, capacity)
    recv_own, recv_partner = (
        lax.all_to_all(sent_own, "grid", split_axis=0, concat_axis=0, tiled=True),
        lax.all_to_all(sent_partner, "grid", split_axis=0, concat_axis=0, tiled=True),
    )
    placed = place_rows(recv_own, placement_matrix(own_map, grid_pos, owned_rows, owners, capacity))
    placed = placed + place_rows(
        recv_partner, placement_matrix(partner_map, grid_pos, owned_rows, owners, capacity)
    )
    front_rows_mine = parent_front[:, 0, :] + placed
    own_panel_cols = front_rows_mine[:, : PW // 2]
    traded = swapped(own_panel_cols.astype(jnp.bfloat16), "cube", 0).astype(own_panel_cols.dtype)
    even_cols = jnp.where(half_index == 0, own_panel_cols, traded)
    odd_cols = jnp.where(half_index == 0, traded, own_panel_cols)
    panel_cols = jnp.stack([even_cols, odd_cols], axis=2).reshape(owned_rows, PW)
    global_rows = grid_pos * owned_rows + lax.iota(jnp.int32, owned_rows)
    picker = (global_rows[:, None] == lax.iota(jnp.int32, PW)[None, :]).astype(jnp.float32)
    top_rows = jnp.einsum(
        "rk,rc->kc",
        picker,
        panel_cols,
        precision=lax.Precision.HIGHEST,
        preferred_element_type=jnp.float32,
    )
    pivot_block = lax.psum(top_rows, "grid")
    lower_factor = jnp.linalg.cholesky(pivot_block)
    factor_mine = lax.linalg.triangular_solve(
        lower_factor, panel_cols, left_side=False, lower=True, transpose_a=True
    )
    update = jnp.einsum(
        "ik,jk->ij",
        factor_mine,
        lax.all_gather(factor_mine, "grid", axis=0, tiled=True),
        precision=lax.Precision.HIGHEST,
        preferred_element_type=jnp.float32,
    )
    my_update = parity_columns(update, half_index)
    schur_rows = front_rows_mine - my_update
    panel_rows = parity_columns(factor_mine, half_index)
    return (schur_rows[:, None, :], panel_rows[:, None, :])


def solution(mesh):
    in_specs = (P("grid", "cube", None), P("cube", "grid", None), P("cube", "grid", None), P())
    out_specs = (P("grid", "cube", None), P("grid", "cube", None))
    return jax.shard_map(shards, mesh=mesh, in_specs=in_specs, out_specs=out_specs, check_vma=False)
```

profile of v0, /device:TPU:0, one launch (start us, length us, event | category | flops | bytes accessed | tf_op | source)
XLA Modules:
  0.0 1541.6 jit_solution(17655353041131905534)
XLA Ops:
  16.6 60.6 %all-gather.3.cloned.1.call-done = bf16[1,6144,512]{2,1,0:T(8,128)(2,1)} async-done(((bf16[1,768,512]{2,1,0:T(8,128)(2,1)}), bf16[1,6144,512]{2,1,0:T(8,128)(2,1)}) %all-gather.3.cloned.1.call-update) | async-done | bytes 6291472 | tf_op jit(solution)/shard_map/all_gather | solution.py:91
  77.2 11.0 fusion.12
  93.7 168.4 %while.14 = (s32[]{:T(128)}, bf16[768,8192]{0,1:T(8,128)(2,1)}, s32[6144]{0:T(1024)S(1)}, bf16[768,6144]{1,0:T(8,128)(2,1)}, s32[]{:T(128)}, /*index=5*/s32[]{:T(128)}, s32[]{:T(128)}, s32[]{:T(128)}) while((s32[]{:T(128)}, bf16[768,8192]{0,1:T(8,128)(2,1)}, s32[6144]{0:T(1024)S(1)}, bf16[768,6144]{1,0:T(8,128)(2,1)}, s32[]{:T(128)}, ...), condition=%wide.region_6.7_spmd, body=%wide.region_5.6_spmd.sunk | while | flops 4838523392 | bytes 10252427 | solution.py:33
  93.7 10.5 fusion.129
  262.1 25.2 %reshape.331 = bf16[768,4096,2]{0,2,1:T(2,128)(2,1)} reshape(bf16[768,8192]{0,1:T(8,128)(2,1)} %get-tuple-element.81) | data formatting | bytes 25165824 | tf_op jit(solution)/shard_map/reshape | solution.py:37
  287.3 29.0 %constant_dynamic-slice_fusion.3 = (bf16[768,4096,1]{0,2,1:T(2,128)(2,1)}, bf16[768,4096,1]{0,2,1:T(2,128)(2,1)}) fusion(bf16[768,4096,2]{0,2,1:T(2,128)(2,1)} %reshape.331, s32[]{:T(128)S(6)} %select_n.128, s32[]{:T(128)S(6)} %select_n.120), kind=kLoop, calls=%fused_computation.201 | loop fusion | bytes 25165832 | tf_op jit(solution)/shard_map/jit(dynamic_index_in_dim)/dynamic_slice | solution.py:38
  316.4 27.3 %copy.53 = bf16[768,4096,1]{1,0,2:T(8,128)(2,1)} copy(bf16[768,4096,1]{0,2,1:T(2,128)(2,1)} %get-tuple-element.125) | data formatting | bytes 12582912 | tf_op jit(solution)/shard_map/jit(dynamic_index_in_dim)/dynamic_slice | solution.py:38
  343.7 15.0 convolution_convert_fusion.1
  364.1 27.1 %copy.63 = bf16[768,4096,1]{1,0,2:T(8,128)(2,1)} copy(bf16[768,4096,1]{0,2,1:T(2,128)(2,1)} %get-tuple-element.124) | data formatting | bytes 12582912 | tf_op jit(solution)/shard_map/jit(dynamic_index_in_dim)/dynamic_slice | solution.py:38
  392.7 136.5 %collective-permute-done = bf16[768,4096]{1,0:T(8,128)(2,1)S(1)} collective-permute-done((bf16[768,4096]{1,0:T(8,128)(2,1)}, bf16[768,4096]{1,0:T(8,128)(2,1)S(1)}, u32[]{:S(2)}, u32[]{:S(2)}) %collective-permute-start) | collective-permute-done | bytes 6291488 | tf_op jit(solution)/shard_map/ppermute | solution.py:16
  529.2 12.5 convolution_convert_fusion
  541.7 96.2 %all-to-all-done = bf16[8,192,4096]{2,1,0:T(8,128)(2,1)} async-done(((bf16[8,192,4096]{2,1,0:T(8,128)(2,1)}), bf16[8,192,4096]{2,1,0:T(8,128)(2,1)}, u32[]{:S(2)}, u32[]{:S(2)}) %all-to-all-start) | async-done | bytes 12582944 | tf_op jit(solution)/shard_map/all_to_all | solution.py:106
  661.2 23.0 %fusion.25 = bf16[1024,1536]{1,0:T(8,128)(2,1)S(1)} fusion(s32[6144]{0:T(1024)S(1)} %get-tuple-element.142, pred[6144,1024]{1,0:T(32,128)(4,1)S(1)} %fusion.123), kind=kOutput, calls=%fused_computation.36 | convolution fusion | flops 19338362880 | bytes 9461760 | tf_op jit(solution)/shard_map/ir,iq->rq/dot_general | solution.py:65
  684.2 23.1 %fusion.22 = bf16[1024,1536]{1,0:T(8,128)(2,1)S(1)} fusion(s32[6144]{0:T(1024)S(1)} %get-tuple-element.141, pred[6144,1024]{1,0:T(32,128)(4,1)S(1)} %fusion.121), kind=kOutput, calls=%fused_computation.35 | convolution fusion | flops 19338362880 | bytes 9461760 | tf_op jit(solution)/shard_map/ir,iq->rq/dot_general | solution.py:65
  707.3 19.5 %fusion.103 = f32[1024,4096]{1,0:T(8,128)} fusion(bf16[1024,1536]{1,0:T(8,128)(2,1)S(1)} %fusion.25, bf16[1536,4096]{1,0:T(8,128)(2,1)} %bitcast.11), kind=kOutput, calls=%fused_computation.220 | convolution fusion | flops 12884901888 | bytes 32505856 | tf_op jit(solution)/shard_map/dot_general | solution.py:72
  726.8 190.2 %all-to-all-done.1 = bf16[8,192,4096]{2,1,0:T(8,128)(2,1)} async-done(((bf16[8,192,4096]{2,1,0:T(8,128)(2,1)}), bf16[8,192,4096]{2,1,0:T(8,128)(2,1)}, u32[]{:S(2)}, u32[]{:S(2)}) %all-to-all-start.1) | async-done | bytes 12582944 | tf_op jit(solution)/shard_map/all_to_all | solution.py:107
  917.0 32.5 %bitcast_add_fusion = f32[1024,4096]{1,0:T(8,128)} fusion(f32[1024,1,4096]{2,1,0:T(1,128)} %param.6, f32[1024,4096]{1,0:T(8,128)} %fusion.103, bf16[1024,1536]{1,0:T(8,128)(2,1)S(1)} %fusion.22, bf16[1536,4096]{1,0:T(8,128)(2,1)} %bitcast.19), kind=kOutput, calls=%fused_computation.22 | convolution fusion | flops 12893290496 | bytes 66060288 | tf_op jit(solution)/shard_map/dot_general | solution.py:72
  952.3 12.0 collective-permute-done.1
  978.8 53.6 %all-reduce.3.cloned.1.call-done = f32[512,512]{0,1:T(8,128)} async-done(((f32[512,512]{0,1:T(8,128)}), f32[512,512]{0,1:T(8,128)}) %all-reduce.3.cloned.1.call-update) | async-done | bytes 1048592 | tf_op jit(solution)/shard_map/psum | solution.py:128
  1037.6 11.7 cholesky.104
  1064.1 11.7 cholesky.217
  1089.4 11.7 cholesky.238
  1114.6 11.7 cholesky.255
  1132.5 14.5 while.15
  1147.0 40.1 %custom-call.33 = f32[4,128,128]{1,2,0:T(8,128)S(1)} custom-call(f32[4,128,128]{2,1,0:T(8,128)} %get-tuple-element.89), custom_call_target="InvertDiagBlocksLowerTriangular" | custom-call | tf_op jit(solution)/shard_map/triangular_solve | solution.py:130
  1208.6 141.4 %all-gather.5.cloned.1.call-done = f32[8192,512]{0,1:T(8,128)} async-done(((f32[1024,512]{0,1:T(8,128)}), f32[8192,512]{0,1:T(8,128)}) %all-gather.5.cloned.1.call-update) | async-done | bytes 16777232 | tf_op jit(solution)/shard_map/all_gather | solution.py:136
  1350.0 59.6 %fusion.97 = f32[1024,8192]{0,1:T(8,128)} fusion(f32[8192,512]{0,1:T(8,128)} %all-gather.5.cloned.1.call-done, f32[1024,128]{0,1:T(8,128)S(1)} %fusion.58, f32[1024,128]{0,1:T(8,128)S(1)} %fusion.59, f32[1024,128]{0,1:T(8,128)S(1)} %fusion.60, f32[1024,128]{0,1:T(8,128)S(1)} %fusion.48), kind=kOutput, calls=%fused_computation.214 | convolution fusion | flops 51541180416 | bytes 52428800 | tf_op jit(solution)/shard_map/ik,jk->ij/dot_general | solution.py:133
  1409.7 39.0 %reshape.339 = f32[1024,4096,2]{0,2,1:T(2,128)} reshape(f32[1024,8192]{0,1:T(8,128)} %fusion.97) | data formatting | bytes 67108864 | tf_op jit(solution)/shard_map/reshape | solution.py:37
  1448.7 17.2 %constant_dynamic-slice_fusion.2 = f32[1024,4096,1]{0,2,1:T(1,128)} fusion(f32[1024,4096,2]{0,2,1:T(2,128)} %reshape.339, s32[]{:T(128)S(6)} %select_n.120), kind=kLoop, calls=%fused_computation.199 | loop fusion | bytes 33554436 | tf_op jit(solution)/shard_map/jit(dynamic_index_in_dim)/dynamic_slice | solution.py:38
  1465.9 37.3 %copy.71 = f32[1024,4096,1]{1,0,2:T(8,128)} copy(f32[1024,4096,1]{0,2,1:T(1,128)} %constant_dynamic-slice_fusion.2) | data formatting | bytes 33554432 | tf_op jit(solution)/shard_map/jit(dynamic_index_in_dim)/dynamic_slice | solution.py:38
  1503.1 11.5 fusion.15
  1514.6 20.2 %copy.73 = f32[1024,1,4096]{2,1,0:T(1,128)} copy(f32[1024,1,4096]{2,0,1:T(8,128)S(1)} %fusion.15) | data formatting | bytes 33554432
  (154 shorter events, 306.2 us)
Async XLA Ops:
  7.2 70.0 %all-gather.3.cloned.1.call-start = ((), (), s32[]{:S(2)}) async-start(), calls=%async_computation.2 | async-start | bytes 7077888 | tf_op jit(solution)/shard_map/all_gather | solution.py:91
  358.7 279.1 %all-to-all-start = ((bf16[8,192,4096]{2,1,0:T(8,128)(2,1)}), bf16[8,192,4096]{2,1,0:T(8,128)(2,1)}, u32[]{:S(2)}, u32[]{:S(2)}) async-start(bf16[8,192,4096]{2,1,0:T(8,128)(2,1)} %bitcast.160), calls=%async_computation | async-start | bytes 25165824 | tf_op jit(solution)/shard_map/all_to_all | solution.py:106
  391.2 138.0 %collective-permute-start = (bf16[768,4096]{1,0:T(8,128)(2,1)}, bf16[768,4096]{1,0:T(8,128)(2,1)S(1)}, u32[]{:S(2)}, u32[]{:S(2)}) collective-permute-start(bf16[768,4096]{1,0:T(8,128)(2,1)} %bitcast.161), channel_id=1, source_target_pairs={{0,8},{8,0},{16,24},{24,16},{1,9},{9,1},{17,25},{25,17},{2,10},{10... | collective-permute-start | bytes 18874376 | tf_op jit(solution)/shard_map/ppermute | solution.py:16
  637.9 279.2 %all-to-all-start.1 = ((bf16[8,192,4096]{2,1,0:T(8,128)(2,1)}), bf16[8,192,4096]{2,1,0:T(8,128)(2,1)}, u32[]{:S(2)}, u32[]{:S(2)}) async-start(bf16[8,192,4096]{2,1,0:T(8,128)(2,1)} %bitcast.159), calls=%async_computation.1 | async-start | bytes 25165824 | tf_op jit(solution)/shard_map/all_to_all | solution.py:107
  643.2 389.1 %all-reduce.3.cloned.1.call-start = ((), (), s32[]{:S(2)}) async-start(), calls=%async_computation.3 | async-start | bytes 2097152 | tf_op jit(solution)/shard_map/psum | solution.py:128
  950.8 13.5 collective-permute-start.1
  974.0 376.0 %all-gather.5.cloned.1.call-start = ((), (), s32[]{:S(2)}) async-start(), calls=%async_computation.4 | async-start | bytes 18874368 | tf_op jit(solution)/shard_map/all_gather | solution.py:136
  1036.6 1.0 copy-start
Sparse Core Ops, SparseCore 0:
  9.6 67.4 all-gather.2
  974.2 58.1 all-reduce.2
  1199.9 150.0 all-gather.4
where the time goes:
time: 1560 us; the launch traced here: 1540 us
  waiting for transfers between devices  691 us (44%)
  matrix products  387 us (25%)
  local copies, waits for them, and re-layouts  271 us (17%)
  other arithmetic  162 us (10%)
  between operations  17 us (1%)
    all_to_all x1, waiting for transfers between devices, shards(): lax.all_to_all(sent_partner, 'grid', split_axis=0, concat_axis=0, tiled=T...  190 us
    dot_general x16, matrix products, place_block(): jnp.dot(contrib_rows, one_hot, preferred_element_type=jnp.float32)  168 us
    ppermute x2, waiting for transfers between devices, swapped(): return lax.ppermute(block, axis, route)  148 us
    dynamic_slice x7, local copies, waits for them, and re-layouts, parity_columns(): return lax.dynamic_index_in_dim(paired, parity, 2, keepdims=False)  143 us
    all_gather x1, waiting for transfers between devices, shards(): lax.all_gather(factor_mine, 'grid', axis=0, tiled=True)  141 us
    all_to_all x1, waiting for transfers between devices, shards(): lax.all_to_all(sent_own, 'grid', split_axis=0, concat_axis=0, tiled=True)  96.2 us
    another operation x15, other arithmetic, shards(): lower_factor = jnp.linalg.cholesky(pivot_block)  81.1 us
    reshape x3, local copies, waits for them, and re-layouts, parity_columns(): paired = matrix.reshape(matrix.shape[0], matrix.shape[1] // 2, 2)  67.6 us
  transfers between devices with their start and end apart: 7, of which 7 were waited for; matrix products, arithmetic and copies ran while one was open for 9% of the time, Pallas kernels for 0%

commit v1 on v0

v1 whole, which is shorter than its diff:
```python
import functools

import jax
import jax.numpy as jnp
from jax import lax
from jax.experimental import pallas as pl
from jax.experimental.pallas import tpu as pltpu
from jax.sharding import PartitionSpec as P

PW = 512
CHUNKS = 4
HIGHEST = lax.Precision.HIGHEST
NT = (((1,), (1,)), ((), ()))
VMEM_LIMIT = 56 * 1024 * 1024


def swapped(block, axis, distance):
    count = lax.axis_size(axis)
    route = []
    for low in range(count):
        high = low | 1 << distance
        if high != low and high < count:
            route += [(low, high), (high, low)]
    return lax.ppermute(block, axis, route)


def one_hot_tile(targets, sources):
    return jnp.where(targets == sources, 1.0, 0.0).astype(jnp.bfloat16)


def spread_kernel(depth, target_ref, map_ref, slab_ref, out_ref):
    total = None
    for step in range(map_ref.shape[0]):
        hot = one_hot_tile(target_ref[...], map_ref[step])
        part = lax.dot_general(
            hot, slab_ref[:, step * depth : (step + 1) * depth], NT, preferred_element_type=jnp.float32
        )
        total = part if total is None else total + part
    out_ref[...] = total.astype(out_ref.dtype)


def spread_rows(slab, child_map, targets, tile):
    depth = slab.shape[1] // 8
    count, width = targets.shape[0], slab.shape[0]
    return pl.pallas_call(
        functools.partial(spread_kernel, depth),
        out_shape=jax.ShapeDtypeStruct((count, width), jnp.bfloat16),
        grid=(count // tile,),
        in_specs=[
            pl.BlockSpec((tile, 1), lambda n: (n, 0)),
            pl.BlockSpec((8, 1, depth), lambda n: (0, 0, 0)),
            pl.BlockSpec(slab.shape, lambda n: (0, 0)),
        ],
        out_specs=pl.BlockSpec((tile, width), lambda n: (n, 0)),
        compiler_params=pltpu.CompilerParams(vmem_limit_bytes=VMEM_LIMIT),
        cost_estimate=pl.CostEstimate(
            flops=2 * count * width * slab.shape[1], bytes_accessed=2 * slab.size + 2 * count * width, transcendentals=0
        ),
    )(targets[:, None], child_map.reshape(8, 1, depth), slab)


def place_kernel(target_ref, map_ref, rows_ref, out_ref):
    total = None
    for source in range(map_ref.shape[0]):
        hot = one_hot_tile(target_ref[...], map_ref[source])
        part = lax.dot_general(hot, rows_ref[source], NT, preferred_element_type=jnp.float32)
        total = part if total is None else total + part
    out_ref[...] = total.T.astype(out_ref.dtype)


def place_columns(received, child_map, targets, tile):
    owners, height, depth = received.shape
    count = targets.shape[0]
    return pl.pallas_call(
        place_kernel,
        out_shape=jax.ShapeDtypeStruct((height, count), jnp.bfloat16),
        grid=(count // tile,),
        in_specs=[
            pl.BlockSpec((tile, 1), lambda n: (n, 0)),
            pl.BlockSpec((owners, 1, depth), lambda n: (0, 0, 0)),
            pl.BlockSpec(received.shape, lambda n: (0, 0, 0)),
        ],
        out_specs=pl.BlockSpec((height, tile), lambda n: (0, n)),
        compiler_params=pltpu.CompilerParams(vmem_limit_bytes=VMEM_LIMIT),
        cost_estimate=pl.CostEstimate(
            flops=2 * received.size * count, bytes_accessed=2 * received.size + 2 * height * count, transcendentals=0
        ),
    )(targets[:, None], child_map.reshape(owners, 1, depth), received)


def dot_exact(left, right, dims=(((1,), (0,)), ((), ()))):
    return lax.dot_general(left, right, dims, precision=HIGHEST, preferred_element_type=jnp.float32)


def inverse_kernel(block, pivot_ref, inverse_ref, work_ref, diag_ref, side_ref):
    order = pivot_ref.shape[0]
    work_ref[...] = pivot_ref[...]
    rows = lax.broadcasted_iota(jnp.int32, (order, order), 0)
    cols = lax.broadcasted_iota(jnp.int32, (order, order), 1)
    inverse_ref[...] = jnp.where(rows == cols, 1.0, 0.0)
    small_rows = lax.broadcasted_iota(jnp.int32, (block, block), 0)
    small_cols = lax.broadcasted_iota(jnp.int32, (block, block), 1)
    row_ids = lax.broadcasted_iota(jnp.int32, (block, 1), 0)
    col_ids = lax.broadcasted_iota(jnp.int32, (1, block), 1)
    for first in range(0, order, block):
        last = first + block
        diag_ref[...] = work_ref[first:last, first:last]
        side_ref[...] = jnp.where(small_rows == small_cols, 1.0, 0.0)

        def eliminate(step, carry):
            diag = diag_ref[...]
            column = jnp.sum(jnp.where(small_cols == step, diag, 0.0), axis=1, keepdims=True)
            pivot_row = diag_ref[pl.ds(step, 1), :]
            side_row = side_ref[pl.ds(step, 1), :]
            pivot = jnp.sum(jnp.where(col_ids == step, pivot_row, 0.0), axis=1, keepdims=True)
            ratio = jnp.where(row_ids > step, column / pivot, 0.0)
            diag_ref[...] = diag - ratio * pivot_row
            side_ref[...] = side_ref[...] - ratio * side_row
            return carry

        lax.fori_loop(0, block, eliminate, 0)
        pivots = jnp.sum(jnp.where(small_rows == small_cols, diag_ref[...], 0.0), axis=1, keepdims=True)
        small_inverse = side_ref[...] / jnp.sqrt(pivots)
        top_work = dot_exact(small_inverse, work_ref[first:last, :])
        top_side = dot_exact(small_inverse, inverse_ref[first:last, :])
        inverse_ref[first:last, :] = top_side
        if last < order:
            below = dot_exact(work_ref[last:, first:last], small_inverse, NT)
            work_ref[last:, :] = work_ref[last:, :] - dot_exact(below, top_work)
            inverse_ref[last:, :] = inverse_ref[last:, :] - dot_exact(below, top_side)


def inverse_factor(pivot):
    order, block = pivot.shape[0], 128
    return pl.pallas_call(
        functools.partial(inverse_kernel, block),
        out_shape=jax.ShapeDtypeStruct((order, order), jnp.float32),
        in_specs=[pl.BlockSpec(memory_space=pltpu.VMEM)],
        out_specs=pl.BlockSpec(memory_space=pltpu.VMEM),
        scratch_shapes=[
            pltpu.VMEM((order, order), jnp.float32),
            pltpu.VMEM((block, block), jnp.float32),
            pltpu.VMEM((block, block), jnp.float32),
        ],
        compiler_params=pltpu.CompilerParams(vmem_limit_bytes=VMEM_LIMIT),
        cost_estimate=pl.CostEstimate(flops=40_000_000_000, bytes_accessed=8 * order * order, transcendentals=0),
    )(pivot)


def two_parts(value):
    high = value.astype(jnp.bfloat16)
    return high, (value - high.astype(jnp.float32)).astype(jnp.bfloat16)


def update_kernel(front_ref, own_ref, other_ref, factor_ref, columns_ref, *rest):
    out_ref = rest[-1]
    high, low = two_parts(factor_ref[...])
    col_high, col_low = two_parts(columns_ref[...])

    def product(left, right):
        return lax.dot_general(left, right, NT, preferred_element_type=jnp.float32)

    term = product(high, col_high) + (product(high, col_low) + product(low, col_high))
    placed = own_ref[...].astype(jnp.float32) + other_ref[...].astype(jnp.float32)
    out_ref[...] = (front_ref[...] + placed) - term


def update_rows(chunk, front, own, other, factor, columns, result, tile):
    rows, width = own.shape
    depth = factor.shape[1]
    front_spec = pl.BlockSpec((rows, tile), lambda n: (chunk, n))
    tile_spec = pl.BlockSpec((rows, tile), lambda n: (0, n))
    in_specs = [
        front_spec,
        tile_spec,
        tile_spec,
        pl.BlockSpec((rows, depth), lambda n: (0, 0)),
        pl.BlockSpec((tile, depth), lambda n: (n, 0)),
    ]
    operands = [front, own, other, factor, columns]
    aliases = {}
    if result is not None:
        in_specs.append(pl.BlockSpec(memory_space=pl.ANY))
        operands.append(result)
        aliases = {5: 0}
    return pl.pallas_call(
        update_kernel,
        out_shape=jax.ShapeDtypeStruct(front.shape, jnp.float32),
        grid=(width // tile,),
        in_specs=in_specs,
        out_specs=front_spec,
        input_output_aliases=aliases,
        compiler_params=pltpu.CompilerParams(vmem_limit_bytes=VMEM_LIMIT),
        cost_estimate=pl.CostEstimate(
            flops=6 * rows * width * depth, bytes_accessed=12 * rows * width + 4 * width * depth, transcendentals=0
        ),
    )(*operands)


def shards(parent_front, child_block, child_panel, row_map):
    owners = lax.axis_size("grid")
    cube_pos = lax.axis_index("cube")
    grid_pos = lax.axis_index("grid")
    half_index = cube_pos % 2
    other_index = 1 - half_index
    owned_rows = parent_front.shape[0]
    half_cols = parent_front.shape[2]
    chunk_rows = owned_rows // CHUNKS
    front = parent_front.reshape(owned_rows, half_cols)
    own_panel = child_panel[0]
    own_map = lax.dynamic_index_in_dim(row_map, cube_pos, 0, keepdims=False)

    own_cols = front[:, : PW // 2]
    partner_cols = swapped(own_cols, "cube", 0)
    pairs, panel_ids = lax.iota(jnp.int32, PW // 2), lax.iota(jnp.int32, PW)
    own_pick = (2 * pairs[:, None] + half_index == panel_ids[None, :]).astype(jnp.float32)
    other_pick = (2 * pairs[:, None] + other_index == panel_ids[None, :]).astype(jnp.float32)
    front_panel = dot_exact(own_cols, own_pick) + dot_exact(partner_cols, other_pick)

    products = jnp.einsum(
        "ik,jk->ij",
        own_panel,
        lax.all_gather(child_panel, "grid", axis=1, tiled=True)[0],
        preferred_element_type=jnp.float32,
    )
    contrib = (child_block[0].astype(jnp.float32) - products).astype(jnp.bfloat16)

    slots = lax.iota(jnp.int32, owners * chunk_rows)
    slot_rows = slots // chunk_rows * owned_rows + slots % chunk_rows
    spread_tile = min(512, owners * chunk_rows)
    column_tile = 512
    received = []
    for chunk in range(CHUNKS):
        sent = spread_rows(contrib, own_map, slot_rows + chunk * chunk_rows, spread_tile)
        sent = sent.reshape(owners, chunk_rows, contrib.shape[0])
        received.append(lax.all_to_all(sent, "grid", split_axis=0, concat_axis=0, tiled=True))

    half_ids = lax.iota(jnp.int32, half_cols)
    panels, owns, others = [], [], []
    for chunk in range(CHUNKS):
        panel_part = place_columns(received[chunk], own_map, panel_ids, column_tile)
        partner_part = swapped(panel_part, "cube", 0)
        base = front_panel[chunk * chunk_rows : (chunk + 1) * chunk_rows]
        panels.append(base + (panel_part.astype(jnp.float32) + partner_part.astype(jnp.float32)))
        outgoing = place_columns(received[chunk], own_map, 2 * half_ids + other_index, column_tile)
        others.append(swapped(outgoing, "cube", 0))
        owns.append(place_columns(received[chunk], own_map, 2 * half_ids + half_index, column_tile))

    top = jnp.zeros((PW, PW), jnp.float32)
    for chunk in range(CHUNKS):
        if chunk * chunk_rows < PW:
            start = grid_pos * owned_rows + chunk * chunk_rows
            inside = start < PW
            at = jnp.where(inside, start, 0)
            kept = lax.dynamic_slice_in_dim(top, at, chunk_rows, 0)
            top = lax.dynamic_update_slice_in_dim(top, jnp.where(inside, panels[chunk], kept), at, 0)
    pivot_block = lax.psum(top, "grid")
    inverse = inverse_factor(pivot_block)
    half_inverse = dot_exact(own_pick, inverse)

    row_ids = lax.iota(jnp.int32, chunk_rows)
    row_pick = (2 * row_ids[: chunk_rows // 2, None] + half_index == row_ids[None, :]).astype(jnp.float32)
    factors, halves, gathered = [], [], []
    for chunk in range(CHUNKS):
        factors.append(dot_exact(panels[chunk], inverse, NT))
        halves.append(dot_exact(panels[chunk], half_inverse, NT))
        mine = dot_exact(row_pick, factors[chunk])
        gathered.append(lax.all_gather(mine, "grid", axis=0, tiled=False))
    columns = jnp.stack(gathered, axis=1).reshape(half_cols, PW)

    schur = None
    for chunk in range(CHUNKS):
        schur = update_rows(
            chunk, front, owns[chunk], others[chunk], factors[chunk], columns, schur, min(1024, half_cols)
        )
    panel_rows = jnp.concatenate(halves, axis=0)
    return (schur[:, None, :], panel_rows[:, None, :])


def solution(mesh):
    in_specs = (P("grid", "cube", None), P("cube", "grid", None), P("cube", "grid", None), P())
    out_specs = (P("grid", "cube", None), P("grid", "cube", None))
    return jax.shard_map(shards, mesh=mesh, in_specs=in_specs, out_specs=out_specs, check_vma=False)
```

time: 1560 us -> 753 us (0.48)
  waiting for transfers between devices: 691 us -> 230 us
  Pallas kernels: 0 us -> 365 us
  matrix products: 387 us -> 27.8 us
  local copies, waits for them, and re-layouts: 271 us -> 59.8 us
  other arithmetic: 162 us -> 14.2 us
    pallas_call x0 -> x21, Pallas kernels: none -> 365 us  [the longest x12 163 us: place_columns(): pl.pallas_call(place_kernel, out_shape=jax.ShapeDtypeStruct((height, coun...]
    dot_general x24 -> x15, matrix products: 357 us -> 16.7 us  [dot_exact(): lax.dot_general(left, right, dims, precision=HIGHEST, preferred_element_t...]
    all_to_all x2 -> x4, waiting for transfers between devices: 286 us -> 90.3 us  [shards(): lax.all_to_all(sent, 'grid', split_axis=0, concat_axis=0, tiled=True)]
    dynamic_slice x9 -> x0, local copies, waits for them, and re-layouts: 146 us -> none  [the longest x7 143 us: parity_columns(): return lax.dynamic_index_in_dim(paired, parity, 2, keepdims=False)]
    all_gather x1 -> x4, waiting for transfers between devices: 141 us -> 0.01 us  [shards(): gathered.append(lax.all_gather(mine, 'grid', axis=0, tiled=False))]
    another operation x29 -> x1, other arithmetic: 134 us -> 6.11 us  [shards(): columns = jnp.stack(gathered, axis=1).reshape(half_cols, PW)]
    ppermute x2 -> x9, waiting for transfers between devices: 148 us -> 36.3 us  [swapped(): return lax.ppermute(block, axis, route)]
    reshape x4 -> x0, local copies, waits for them, and re-layouts: 70.3 us -> none  [the longest x3 67.6 us: parity_columns(): paired = matrix.reshape(matrix.shape[0], matrix.shape[1] // 2, 2)]
  transfers between devices with their start and end apart: 7 -> 19, of which waited for: 7 -> 8; matrix products, arithmetic and copies ran while one was open for 9% -> 8% of each run, Pallas kernels for 0% -> 45%
where the time goes in v1:
time: 753 us; the launch traced here: 739 us
  Pallas kernels  365 us (48%)
  waiting for transfers between devices  230 us (31%)
  local copies, waits for them, and re-layouts  59.8 us (8%)
  starting transfers between devices  28.2 us (4%)
  matrix products  27.8 us (4%)
  between operations  14.7 us (2%)
  other arithmetic  14.2 us (2%)
    pallas_call x12, Pallas kernels, place_columns(): pl.pallas_call(place_kernel, out_shape=jax.ShapeDtypeStruct((height, coun...  163 us
    pallas_call x4, Pallas kernels, spread_rows(): pl.pallas_call(functools.partial(spread_kernel, depth), out_shape=jax.Sha...  101 us
    all_to_all x4, waiting for transfers between devices, shards(): lax.all_to_all(sent, 'grid', split_axis=0, concat_axis=0, tiled=True)  90.3 us
    all_gather x1, waiting for transfers between devices, shards(): lax.all_gather(child_panel, 'grid', axis=1, tiled=True)[0]  67.4 us
    pallas_call x1, Pallas kernels, inverse_factor(): pl.pallas_call(functools.partial(inverse_kernel, block), out_shape=jax.Sh...  61.3 us
    unnamed x65, local copies, waits for them, and re-layouts  56 us
    pallas_call x4, Pallas kernels, update_rows(): pl.pallas_call(update_kernel, out_shape=jax.ShapeDtypeStruct(front.shape,...  39.6 us
    ppermute x9, waiting for transfers between devices, swapped(): return lax.ppermute(block, axis, route)  36.3 us
  transfers between devices with their start and end apart: 19, of which 8 were waited for; matrix products, arithmetic and copies ran while one was open for 8% of the time, Pallas kernels for 45%

profile of v1, /device:TPU:0, one launch (start us, length us, event | category | flops | bytes accessed | tf_op | source)
XLA Modules:
  0.0 739.3 jit_solution(9397872866225840055)
XLA Ops:
  9.7 67.4 %all-gather.10.cloned.1.call-done = bf16[1,6144,512]{2,1,0:T(8,128)(2,1)} async-done(((bf16[1,768,512]{2,1,0:T(8,128)(2,1)}), bf16[1,6144,512]{2,1,0:T(8,128)(2,1)}) %all-gather.10.cloned.1.call-update) | async-done | bytes 6291472 | tf_op jit(solution)/shard_map/all_gather | solution.py:223
  77.1 11.0 %fusion.slab_ref = bf16[768,6144]{1,0:T(8,128)(2,1)} fusion(bf16[1,768,6144]{2,1,0:T(8,128)(2,1)} %param.5, bf16[1,6144,512]{2,1,0:T(8,128)(2,1)} %all-gather.10.cloned.1.call-done, bf16[1,768,512]{2,1,0:T(8,128)(2,1)} %param.6), kind=kOutput, calls=%fused_computation.1 | convolution fusion | flops 4845993984 | bytes 25952256 | tf_op jit(solution)/shard_map/ik,jk->ij/dot_general | solution.py:220
  88.2 25.2 %shard_map.65 = bf16[2048,768]{1,0:T(8,128)(2,1)} custom-call(s32[2048,1]{1,0:T(8,128)} %broadcast_add_fusion.2.target_ref, s32[8,1,768]{2,1,0:T(1,128)} %bitcast.68, bf16[768,6144]{1,0:T(8,128)(2,1)} %fusion.slab_ref), custom_call_target="tpu_custom_call" | custom-call | flops 19327352832 | bytes 12582912 | tf_op jit(solution)/shard_map/pallas_call | solution.py:45
  118.2 25.1 %shard_map.63 = bf16[2048,768]{1,0:T(8,128)(2,1)} custom-call(s32[2048,1]{1,0:T(8,128)} %fusion.11.target_ref, s32[8,1,768]{2,1,0:T(1,128)} %bitcast.69, bf16[768,6144]{1,0:T(8,128)(2,1)} %fusion.slab_ref), custom_call_target="tpu_custom_call" | custom-call | flops 19327352832 | bytes 12582912 | tf_op jit(solution)/shard_map/pallas_call | solution.py:45
  143.3 45.2 %all-to-all-done.2.rows_ref = bf16[8,256,768]{2,1,0:T(8,128)(2,1)S(1)} async-done(((bf16[8,256,768]{2,1,0:T(8,128)(2,1)}), bf16[8,256,768]{2,1,0:T(8,128)(2,1)S(1)}, u32[]{:S(2)}, u32[]{:S(2)}) %all-to-all-start.2) | async-done | bytes 3145760 | tf_op jit(solution)/shard_map/all_to_all | solution.py:236
  195.5 25.2 %shard_map.59 = bf16[2048,768]{1,0:T(8,128)(2,1)} custom-call(s32[2048,1]{1,0:T(8,128)} %broadcast_add_fusion.1.target_ref, s32[8,1,768]{2,1,0:T(1,128)} %bitcast.70, bf16[768,6144]{1,0:T(8,128)(2,1)} %fusion.slab_ref), custom_call_target="tpu_custom_call" | custom-call | flops 19327352832 | bytes 12582912 | tf_op jit(solution)/shard_map/pallas_call | solution.py:45
  220.6 45.1 %all-to-all-done.1.rows_ref = bf16[8,256,768]{2,1,0:T(8,128)(2,1)S(1)} async-done(((bf16[8,256,768]{2,1,0:T(8,128)(2,1)}), bf16[8,256,768]{2,1,0:T(8,128)(2,1)S(1)}, u32[]{:S(2)}, u32[]{:S(2)}) %all-to-all-start.1) | async-done | bytes 3145760 | tf_op jit(solution)/shard_map/all_to_all | solution.py:236
  272.0 19.1 %copy.21 = f32[1024,1,4096]{2,0,1:T(8,128)S(1)} copy(f32[1024,1,4096]{2,1,0:T(1,128)} %param.4) | data formatting | bytes 33554432
  291.1 6.2 copy-done.2
  303.2 4.6 shard_map.64
  308.4 15.1 %collective-permute-done.1 = f32[1024,256]{1,0:T(8,128)S(1)} collective-permute-done((f32[1024,256]{1,0:T(8,128)S(1)}, f32[1024,256]{1,0:T(8,128)S(1)}, u32[]{:S(2)}, u32[]{:S(2)}) %collective-permute-start.1) | collective-permute-done | bytes 1048608 | tf_op jit(solution)/shard_map/ppermute | solution.py:24
  325.3 4.6 shard_map.66
  332.1 5.2 collective-permute-done.4
  339.2 25.3 %shard_map.68 = bf16[2048,768]{1,0:T(8,128)(2,1)} custom-call(s32[2048,1]{1,0:T(8,128)} %broadcast_add_fusion.target_ref, s32[8,1,768]{2,1,0:T(1,128)} %bitcast.73, bf16[768,6144]{1,0:T(8,128)(2,1)} %fusion.slab_ref), custom_call_target="tpu_custom_call" | custom-call | flops 19327352832 | bytes 12582912 | tf_op jit(solution)/shard_map/pallas_call | solution.py:45
  375.9 34.8 %all-reduce.2.cloned.1.call-done.pivot_ref = f32[512,512]{1,0:T(8,128)} async-done(((f32[512,512]{1,0:T(8,128)}), f32[512,512]{1,0:T(8,128)}) %all-reduce.2.cloned.1.call-update) | async-done | bytes 1048592 | tf_op jit(solution)/shard_map/psum | solution.py:257
  410.7 61.3 %shard_map.67 = f32[512,512]{1,0:T(8,128)} custom-call(f32[512,512]{1,0:T(8,128)} %all-reduce.2.cloned.1.call-done.pivot_ref), custom_call_target="tpu_custom_call" | custom-call | flops 40000000000 | bytes 2097152 | tf_op jit(solution)/shard_map/pallas_call | solution.py:135
  478.9 4.6 shard_map.69
  493.9 18.1 %shard_map.75 = bf16[256,4096]{1,0:T(8,128)(2,1)} custom-call(s32[4096,1]{1,0:T(8,128)} %fusion.6.target_ref, s32[8,1,768]{2,1,0:T(1,128)} %bitcast.76, bf16[8,256,768]{2,1,0:T(8,128)(2,1)} %copy-done.9), custom_call_target="tpu_custom_call" | custom-call | flops 12884901888 | bytes 5242880 | tf_op jit(solution)/shard_map/pallas_call | solution.py:74
  513.4 18.1 %shard_map.61 = bf16[256,4096]{1,0:T(8,128)(2,1)} custom-call(s32[4096,1]{1,0:T(8,128)} %fusion.6.target_ref, s32[8,1,768]{2,1,0:T(1,128)} %bitcast.77, bf16[8,256,768]{2,1,0:T(8,128)(2,1)} %all-to-all-done.rows_ref), custom_call_target="tpu_custom_call" | custom-call | flops 12884901888 | bytes 5242880 | tf_op jit(solution)/shard_map/pallas_call | solution.py:74
  532.1 18.1 %shard_map.73 = bf16[256,4096]{1,0:T(8,128)(2,1)} custom-call(s32[4096,1]{1,0:T(8,128)} %fusion.6.target_ref, s32[8,1,768]{2,1,0:T(1,128)} %bitcast.78, bf16[8,256,768]{2,1,0:T(8,128)(2,1)} %copy-done.10), custom_call_target="tpu_custom_call" | custom-call | flops 12884901888 | bytes 5242880 | tf_op jit(solution)/shard_map/pallas_call | solution.py:74
  555.1 18.1 %shard_map.71 = bf16[256,4096]{1,0:T(8,128)(2,1)} custom-call(s32[4096,1]{1,0:T(8,128)} %fusion.6.target_ref, s32[8,1,768]{2,1,0:T(1,128)} %bitcast.79, bf16[8,256,768]{2,1,0:T(8,128)(2,1)} %all-to-all-done.3.rows_ref), custom_call_target="tpu_custom_call" | custom-call | flops 12884901888 | bytes 5242880 | tf_op jit(solution)/shard_map/pallas_call | solution.py:74
  573.8 18.1 %shard_map.70.own_ref = bf16[256,4096]{1,0:T(8,128)(2,1)} custom-call(s32[4096,1]{1,0:T(8,128)} %fusion.7.target_ref, s32[8,1,768]{2,1,0:T(1,128)} %bitcast.80, bf16[8,256,768]{2,1,0:T(8,128)(2,1)} %all-to-all-done.3.rows_ref), custom_call_target="tpu_custom_call" | custom-call | flops 12884901888 | bytes 5242880 | tf_op jit(solution)/shard_map/pallas_call | solution.py:74
  591.9 18.1 %shard_map.72.own_ref = bf16[256,4096]{1,0:T(8,128)(2,1)} custom-call(s32[4096,1]{1,0:T(8,128)} %fusion.7.target_ref, s32[8,1,768]{2,1,0:T(1,128)} %bitcast.81, bf16[8,256,768]{2,1,0:T(8,128)(2,1)} %copy-done.10), custom_call_target="tpu_custom_call" | custom-call | flops 12884901888 | bytes 5242880 | tf_op jit(solution)/shard_map/pallas_call | solution.py:74
  613.0 18.1 %shard_map.60.own_ref = bf16[256,4096]{1,0:T(8,128)(2,1)} custom-call(s32[4096,1]{1,0:T(8,128)} %fusion.7.target_ref, s32[8,1,768]{2,1,0:T(1,128)} %bitcast.82, bf16[8,256,768]{2,1,0:T(8,128)(2,1)} %all-to-all-done.rows_ref), custom_call_target="tpu_custom_call" | custom-call | flops 12884901888 | bytes 5242880 | tf_op jit(solution)/shard_map/pallas_call | solution.py:74
  631.1 18.3 %shard_map.74.own_ref = bf16[256,4096]{1,0:T(8,128)(2,1)} custom-call(s32[4096,1]{1,0:T(8,128)} %fusion.7.target_ref, s32[8,1,768]{2,1,0:T(1,128)} %bitcast.83, bf16[8,256,768]{2,1,0:T(8,128)(2,1)} %copy-done.9), custom_call_target="tpu_custom_call" | custom-call | flops 12884901888 | bytes 5242880 | tf_op jit(solution)/shard_map/pallas_call | solution.py:74
  655.1 6.1 pad_maximum_fusion
  661.2 9.9 %shard_map.76.rest_0_ = f32[1024,4096]{1,0:T(8,128)} custom-call(f32[1024,4096]{1,0:T(8,128)} %bitcast.51, bf16[256,4096]{1,0:T(8,128)(2,1)} %shard_map.74.own_ref, bf16[256,4096]{1,0:T(8,128)(2,1)} %collective-permute-done.8.other_ref, f32[256,512]{1,0:T(8,128)} %copy-done.8, f32[4096,512]{1,0:T(8,128)} %bitcast.56), custom_call_target="tpu_custom_call" | custom-call | flops 3221225472 | bytes 20971520 | tf_op jit(solution)/shard_map/pallas_call | solution.py:186
  671.1 9.9 %shard_map.77.rest_0_ = f32[1024,4096]{1,0:T(8,128)} custom-call(f32[1024,4096]{1,0:T(8,128)} %bitcast.52, bf16[256,4096]{1,0:T(8,128)(2,1)} %shard_map.72.own_ref, bf16[256,4096]{1,0:T(8,128)(2,1)} %collective-permute-done.7.other_ref, f32[256,512]{1,0:T(8,128)} %copy-done.7, f32[4096,512]{1,0:T(8,128)} %bitcast.57, ...), custom_call_target="tpu_custom_call", output_to_operand_aliasing={{}: (5, {})} | custom-call | flops 3221225472 | bytes 20971520 | tf_op jit(solution)/shard_map/pallas_call | solution.py:186
  681.0 11.7 %collective-permute-done.6.other_ref = bf16[256,4096]{1,0:T(8,128)(2,1)} collective-permute-done((bf16[256,4096]{1,0:T(8,128)(2,1)}, bf16[256,4096]{1,0:T(8,128)(2,1)}, u32[]{:S(2)}, u32[]{:S(2)}) %collective-permute-start.6) | collective-permute-done | bytes 2097184 | tf_op jit(solution)/shard_map/ppermute | solution.py:24
  692.7 9.9 %shard_map.78.rest_0_ = f32[1024,4096]{1,0:T(8,128)} custom-call(f32[1024,4096]{1,0:T(8,128)} %bitcast.53, bf16[256,4096]{1,0:T(8,128)(2,1)} %shard_map.70.own_ref, bf16[256,4096]{1,0:T(8,128)(2,1)} %collective-permute-done.6.other_ref, f32[256,512]{1,0:T(8,128)} %copy-done.6, f32[4096,512]{1,0:T(8,128)} %bitcast.58, ...), custom_call_target="tpu_custom_call", output_to_operand_aliasing={{}: (5, {})} | custom-call | flops 3221225472 | bytes 20971520 | tf_op jit(solution)/shard_map/pallas_call | solution.py:186
  702.5 9.9 %shard_map.79 = f32[1024,4096]{1,0:T(8,128)} custom-call(f32[1024,4096]{1,0:T(8,128)} %bitcast.54, bf16[256,4096]{1,0:T(8,128)(2,1)} %shard_map.60.own_ref, bf16[256,4096]{1,0:T(8,128)(2,1)} %collective-permute-done.other_ref, f32[256,512]{1,0:T(8,128)} %copy-done.5, f32[4096,512]{1,0:T(8,128)} %bitcast.59, ...), custom_call_target="tpu_custom_call", output_to_operand_aliasing={{}: (5, {})} | custom-call | flops 3221225472 | bytes 20971520 | tf_op jit(solution)/shard_map/pallas_call | solution.py:186
  712.4 19.9 %copy.15 = f32[1024,1,4096]{2,1,0:T(1,128)} copy(f32[1024,1,4096]{2,0,1:T(8,128)} %bitcast.55) | data formatting | bytes 33554432
  (135 shorter events, 77.3 us)
Async XLA Ops:
  7.2 70.0 %all-gather.10.cloned.1.call-start = ((), (), s32[]{:S(2)}) async-start(), calls=%async_computation.4 | async-start | bytes 7077888 | tf_op jit(solution)/shard_map/all_gather | solution.py:223
  113.4 75.1 %all-to-all-start.2 = ((bf16[8,256,768]{2,1,0:T(8,128)(2,1)}), bf16[8,256,768]{2,1,0:T(8,128)(2,1)S(1)}, u32[]{:S(2)}, u32[]{:S(2)}) async-start(bf16[8,256,768]{2,1,0:T(8,128)(2,1)} %bitcast.63), calls=%async_computation.2 | async-start | bytes 6291456 | tf_op jit(solution)/shard_map/all_to_all | solution.py:236
  190.2 75.6 %all-to-all-start.1 = ((bf16[8,256,768]{2,1,0:T(8,128)(2,1)}), bf16[8,256,768]{2,1,0:T(8,128)(2,1)S(1)}, u32[]{:S(2)}, u32[]{:S(2)}) async-start(bf16[8,256,768]{2,1,0:T(8,128)(2,1)} %bitcast.62), calls=%async_computation.1 | async-start | bytes 6291456 | tf_op jit(solution)/shard_map/all_to_all | solution.py:236
  267.5 97.0 %all-to-all-start = ((bf16[8,256,768]{2,1,0:T(8,128)(2,1)}), bf16[8,256,768]{2,1,0:T(8,128)(2,1)}, u32[]{:S(2)}, u32[]{:S(2)}) async-start(bf16[8,256,768]{2,1,0:T(8,128)(2,1)} %bitcast.60), calls=%async_computation | async-start | bytes 6291456 | tf_op jit(solution)/shard_map/all_to_all | solution.py:236
  271.9 138.8 %all-reduce.2.cloned.1.call-start = ((), (), s32[]{:S(2)}) async-start(), calls=%async_computation.5 | async-start | bytes 2097152 | tf_op jit(solution)/shard_map/psum | solution.py:257
  291.1 6.2 copy-start.2
  297.4 26.0 %collective-permute-start.1 = (f32[1024,256]{1,0:T(8,128)S(1)}, f32[1024,256]{1,0:T(8,128)S(1)}, u32[]{:S(2)}, u32[]{:S(2)}) collective-permute-start(f32[1024,256]{1,0:T(8,128)S(1)} %slice.24), channel_id=1, source_target_pairs={{0,8},{8,0},{16,24},{24,16},{1,9},{9,1},{17,25},{25,17},{2,10},{10... | collective-permute-start | bytes 3145736 | tf_op jit(solution)/shard_map/ppermute | solution.py:24
  307.8 23.6 %collective-permute-start.3 = (bf16[256,512]{1,0:T(8,128)(2,1)}, bf16[256,512]{1,0:T(8,128)(2,1)S(1)}, u32[]{:S(2)}, u32[]{:S(2)}) collective-permute-start(bf16[256,512]{1,0:T(8,128)(2,1)} %shard_map.64), channel_id=1, source_target_pairs={{0,8},{8,0},{16,24},{24,16},{1,9},{9,1},{17,25},{25,17},{2,10},{10... | collective-permute-start | bytes 786440 | tf_op jit(solution)/shard_map/ppermute | solution.py:24
  325.3 6.2 copy-start.11
  329.9 8.1 %copy-start.16 = (bf16[256,512]{1,0:T(8,128)(2,1)S(1)}, bf16[256,512]{1,0:T(8,128)(2,1)}, u32[]{:S(2)}) copy-start(bf16[256,512]{1,0:T(8,128)(2,1)} %shard_map.66) | copy-start | bytes 786436
  329.9 7.4 collective-permute-start.4
  364.5 113.7 %all-to-all-start.3 = ((bf16[8,256,768]{2,1,0:T(8,128)(2,1)}), bf16[8,256,768]{2,1,0:T(8,128)(2,1)}, u32[]{:S(2)}, u32[]{:S(2)}) async-start(bf16[8,256,768]{2,1,0:T(8,128)(2,1)} %bitcast.61), calls=%async_computation.3 | async-start | bytes 6291456 | tf_op jit(solution)/shard_map/all_to_all | solution.py:236
  369.1 286.0 %all-gather.18.cloned.1.call-start = ((), (), s32[]{:S(2)}) async-start(), calls=%async_computation.9 | async-start | bytes 2359296 | tf_op jit(solution)/shard_map/all_gather | solution.py:268
  374.4 97.6 %copy-start.21 = (bf16[256,512]{1,0:T(8,128)(2,1)S(1)}, bf16[256,512]{1,0:T(8,128)(2,1)}, u32[]{:S(2)}) copy-start(bf16[256,512]{1,0:T(8,128)(2,1)} %shard_map.62) | copy-start | bytes 786436
  374.4 97.6 %collective-permute-start.2 = (bf16[256,512]{1,0:T(8,128)(2,1)}, bf16[256,512]{1,0:T(8,128)(2,1)S(1)}, u32[]{:S(2)}, u32[]{:S(2)}) collective-permute-start(bf16[256,512]{1,0:T(8,128)(2,1)} %shard_map.62), channel_id=1, source_target_pairs={{0,8},{8,0},{16,24},{24,16},{1,9},{9,1},{17,25},{25,17},{2,10},{10... | collective-permute-start | bytes 786440 | tf_op jit(solution)/shard_map/ppermute | solution.py:24
  476.3 178.7 %all-gather.16.cloned.1.call-start = ((), (), s32[]{:S(2)}) async-start(), calls=%async_computation.8 | async-start | bytes 2359296 | tf_op jit(solution)/shard_map/all_gather | solution.py:268
  483.5 7.3 copy-start.3
  483.5 7.3 copy-start.25
  483.5 7.3 collective-permute-start.5
  493.8 161.2 %all-gather.14.cloned.1.call-start = ((), (), s32[]{:S(2)}) async-start(), calls=%async_computation.7 | async-start | bytes 2359296 | tf_op jit(solution)/shard_map/all_gather | solution.py:268
  512.0 149.1 %collective-permute-start.8 = (bf16[256,4096]{1,0:T(8,128)(2,1)}, bf16[256,4096]{1,0:T(8,128)(2,1)}, u32[]{:S(2)}, u32[]{:S(2)}) collective-permute-start(bf16[256,4096]{1,0:T(8,128)(2,1)} %shard_map.75), channel_id=1, source_target_pairs={{0,8},{8,0},{16,24},{24,16},{1,9},{9,1},{17,25},{25,17},{2,10},{10... | collective-permute-start | bytes 6291464 | tf_op jit(solution)/shard_map/ppermute | solution.py:24
  531.5 20.1 %copy-start.19 = (bf16[256,512]{1,0:T(8,128)(2,1)S(1)}, bf16[256,512]{1,0:T(8,128)(2,1)}, u32[]{:S(2)}) copy-start(bf16[256,512]{1,0:T(8,128)(2,1)} %copy-done.18) | copy-start | bytes 786436
  531.5 171.1 %collective-permute-start = (bf16[256,4096]{1,0:T(8,128)(2,1)}, bf16[256,4096]{1,0:T(8,128)(2,1)}, u32[]{:S(2)}, u32[]{:S(2)}) collective-permute-start(bf16[256,4096]{1,0:T(8,128)(2,1)} %shard_map.61), channel_id=1, source_target_pairs={{0,8},{8,0},{16,24},{24,16},{1,9},{9,1},{17,25},{25,17},{2,10},{10... | collective-permute-start | bytes 6291464 | tf_op jit(solution)/shard_map/ppermute | solution.py:24
  550.2 120.8 %collective-permute-start.7 = (bf16[256,4096]{1,0:T(8,128)(2,1)}, bf16[256,4096]{1,0:T(8,128)(2,1)}, u32[]{:S(2)}, u32[]{:S(2)}) collective-permute-start(bf16[256,4096]{1,0:T(8,128)(2,1)} %shard_map.73), channel_id=1, source_target_pairs={{0,8},{8,0},{16,24},{24,16},{1,9},{9,1},{17,25},{25,17},{2,10},{10... | collective-permute-start | bytes 6291464 | tf_op jit(solution)/shard_map/ppermute | solution.py:24
  554.6 100.5 %all-gather.12.cloned.1.call-start = ((), (), s32[]{:S(2)}) async-start(), calls=%async_computation.6 | async-start | bytes 2359296 | tf_op jit(solution)/shard_map/all_gather | solution.py:268
  573.1 119.5 %collective-permute-start.6 = (bf16[256,4096]{1,0:T(8,128)(2,1)}, bf16[256,4096]{1,0:T(8,128)(2,1)}, u32[]{:S(2)}, u32[]{:S(2)}) collective-permute-start(bf16[256,4096]{1,0:T(8,128)(2,1)} %shard_map.71), channel_id=1, source_target_pairs={{0,8},{8,0},{16,24},{24,16},{1,9},{9,1},{17,25},{25,17},{2,10},{10... | collective-permute-start | bytes 6291464 | tf_op jit(solution)/shard_map/ppermute | solution.py:24
  591.9 18.1 %copy-start.12 = (bf16[256,512]{1,0:T(8,128)(2,1)S(1)}, bf16[256,512]{1,0:T(8,128)(2,1)}, u32[]{:S(2)}) copy-start(bf16[256,512]{1,0:T(8,128)(2,1)} %shard_map.64) | copy-start | bytes 786436
  591.9 18.1 %copy-start.14 = (bf16[256,512]{1,0:T(8,128)(2,1)S(1)}, bf16[256,512]{1,0:T(8,128)(2,1)}, u32[]{:S(2)}) copy-start(bf16[256,512]{1,0:T(8,128)(2,1)} %copy-done.13) | copy-start | bytes 786436
  631.1 18.3 %copy-start.30 = (s32[256]{0:T(256)S(1)}, s32[256]{0:T(256)}, u32[]{:S(2)}) copy-start(s32[256]{0:T(256)} %copy-done.29) | copy-start | bytes 3076
  631.1 19.1 %copy-start.22 = (bf16[256,512]{1,0:T(8,128)(2,1)S(1)}, bf16[256,512]{1,0:T(8,128)(2,1)}, u32[]{:S(2)}) copy-start(bf16[256,512]{1,0:T(8,128)(2,1)} %shard_map.62) | copy-start | bytes 786436
  631.1 19.1 %copy-start.24 = (bf16[256,512]{1,0:T(8,128)(2,1)S(1)}, bf16[256,512]{1,0:T(8,128)(2,1)}, u32[]{:S(2)}) copy-start(bf16[256,512]{1,0:T(8,128)(2,1)} %copy-done.23) | copy-start | bytes 786436
  712.4 19.9 %copy-start.1 = (s32[4,6144]{1,0:T(4,128)S(1)}, s32[4,6144]{1,0:T(4,128)}, u32[]{:S(2)}) copy-start(s32[4,6144]{1,0:T(4,128)} %param.7) | copy-start | bytes 294916
  (18 other events, 28.8 us)
Sparse Core Ops, SparseCore 0:
  9.7 67.4 all-gather.9
  339.3 71.3 all-reduce.1
  476.4 34.1 all-gather.17
  512.1 28.5 all-gather.15
  554.7 34.7 all-gather.13
  613.1 35.6 all-gather.11

commit v2 on v1

--- a/solution.py
+++ b/solution.py
@@ -8,6 +8,7 @@
 from jax.sharding import PartitionSpec as P
 
 PW = 512
+LANES = 128
 CHUNKS = 4
 HIGHEST = lax.Precision.HIGHEST
 NT = (((1,), (1,)), ((), ()))
@@ -28,8 +29,8 @@
     return jnp.where(targets == sources, 1.0, 0.0).astype(jnp.bfloat16)
 
 
-def spread_kernel(depth, target_ref, map_ref, slab_ref, out_ref):
-    total = None
+def spread_kernel(depth, target_ref, map_ref, slab_ref, *rest):
+    out_ref, total = rest[-1], None
     for step in range(map_ref.shape[0]):
         hot = one_hot_tile(target_ref[...], map_ref[step])
         part = lax.dot_general(
@@ -39,7 +40,7 @@
     out_ref[...] = total.astype(out_ref.dtype)
 
 
-def spread_rows(slab, child_map, targets, tile):
+def spread_rows(slab, child_map, targets, tile, after=()):
     depth = slab.shape[1] // 8
     count, width = targets.shape[0], slab.shape[0]
     return pl.pallas_call(
@@ -50,17 +51,18 @@
             pl.BlockSpec((tile, 1), lambda n: (n, 0)),
             pl.BlockSpec((8, 1, depth), lambda n: (0, 0, 0)),
             pl.BlockSpec(slab.shape, lambda n: (0, 0)),
-        ],
+        ]
+        + [pl.BlockSpec(memory_space=pl.ANY)] * len(after),
         out_specs=pl.BlockSpec((tile, width), lambda n: (n, 0)),
         compiler_params=pltpu.CompilerParams(vmem_limit_bytes=VMEM_LIMIT),
         cost_estimate=pl.CostEstimate(
             flops=2 * count * width * slab.shape[1], bytes_accessed=2 * slab.size + 2 * count * width, transcendentals=0
         ),
-    )(targets[:, None], child_map.reshape(8, 1, depth), slab)
-
-
-def place_kernel(target_ref, map_ref, rows_ref, out_ref):
-    total = None
+    )(targets[:, None], child_map.reshape(8, 1, depth), slab, *after)
+
+
+def place_kernel(target_ref, map_ref, rows_ref, *rest):
+    out_ref, total = rest[-1], None
     for source in range(map_ref.shape[0]):
         hot = one_hot_tile(target_ref[...], map_ref[source])
         part = lax.dot_general(hot, rows_ref[source], NT, preferred_element_type=jnp.float32)
@@ -68,7 +70,7 @@
     out_ref[...] = total.T.astype(out_ref.dtype)
 
 
-def place_columns(received, child_map, targets, tile):
+def place_columns(received, child_map, targets, tile, after=()):
     owners, height, depth = received.shape
     count = targets.shape[0]
     return pl.pallas_call(
@@ -79,20 +81,22 @@
             pl.BlockSpec((tile, 1), lambda n: (n, 0)),
             pl.BlockSpec((owners, 1, depth), lambda n: (0, 0, 0)),
             pl.BlockSpec(received.shape, lambda n: (0, 0, 0)),
-        ],
+        ]
+        + [pl.BlockSpec(memory_space=pl.ANY)] * len(after),
         out_specs=pl.BlockSpec((height, tile), lambda n: (0, n)),
         compiler_params=pltpu.CompilerParams(vmem_limit_bytes=VMEM_LIMIT),
         cost_estimate=pl.CostEstimate(
             flops=2 * received.size * count, bytes_accessed=2 * received.size + 2 * height * count, transcendentals=0
         ),
-    )(targets[:, None], child_map.reshape(owners, 1, depth), received)
+    )(targets[:, None], child_map.reshape(owners, 1, depth), received, *after)
 
 
 def dot_exact(left, right, dims=(((1,), (0,)), ((), ()))):
     return lax.dot_general(left, right, dims, precision=HIGHEST, preferred_element_type=jnp.float32)
 
 
-def inverse_kernel(block, pivot_ref, inverse_ref, work_ref, diag_ref, side_ref):
+def inverse_kernel(block, pivot_ref, *rest):
+    inverse_ref, work_ref, diag_ref, side_ref = rest[-4:]
     order = pivot_ref.shape[0]
     work_ref[...] = pivot_ref[...]
     rows = lax.broadcasted_iota(jnp.int32, (order, order), 0)
@@ -130,12 +134,12 @@
             inverse_ref[last:, :] = inverse_ref[last:, :] - dot_exact(below, top_side)
 
 
-def inverse_factor(pivot):
+def inverse_factor(pivot, after):
     order, block = pivot.shape[0], 128
     return pl.pallas_call(
         functools.partial(inverse_kernel, block),
         out_shape=jax.ShapeDtypeStruct((order, order), jnp.float32),
-        in_specs=[pl.BlockSpec(memory_space=pltpu.VMEM)],
+        in_specs=[pl.BlockSpec(memory_space=pltpu.VMEM)] + [pl.BlockSpec(memory_space=pl.ANY)] * len(after),
         out_specs=pl.BlockSpec(memory_space=pltpu.VMEM),
         scratch_shapes=[
             pltpu.VMEM((order, order), jnp.float32),
@@ -144,7 +148,7 @@
         ],
         compiler_params=pltpu.CompilerParams(vmem_limit_bytes=VMEM_LIMIT),
         cost_estimate=pl.CostEstimate(flops=40_000_000_000, bytes_accessed=8 * order * order, transcendentals=0),
-    )(pivot)
+    )(pivot, *after)
 
 
 def two_parts(value):
@@ -162,7 +166,9 @@
 
     term = product(high, col_high) + (product(high, col_low) + product(low, col_high))
     placed = own_ref[...].astype(jnp.float32) + other_ref[...].astype(jnp.float32)
-    out_ref[...] = (front_ref[...] + placed) - term
+    value = (front_ref[...] + placed) - term
+    for part in range(out_ref.shape[1]):
+        out_ref[:, part, :] = value[:, part * LANES : (part + 1) * LANES]
 
 
 def update_rows(chunk, front, own, other, factor, columns, result, tile):
@@ -185,10 +191,10 @@
         aliases = {5: 0}
     return pl.pallas_call(
         update_kernel,
-        out_shape=jax.ShapeDtypeStruct(front.shape, jnp.float32),
+        out_shape=jax.ShapeDtypeStruct((front.shape[0], width // LANES, LANES), jnp.float32),
         grid=(width // tile,),
         in_specs=in_specs,
-        out_specs=front_spec,
+        out_specs=pl.BlockSpec((rows, tile // LANES, LANES), lambda n: (chunk, n, 0)),
         input_output_aliases=aliases,
         compiler_params=pltpu.CompilerParams(vmem_limit_bytes=VMEM_LIMIT),
         cost_estimate=pl.CostEstimate(
@@ -229,44 +235,71 @@
     slot_rows = slots // chunk_rows * owned_rows + slots % chunk_rows
     spread_tile = min(512, owners * chunk_rows)
     column_tile = 512
-    received = []
-    for chunk in range(CHUNKS):
-        sent = spread_rows(contrib, own_map, slot_rows + chunk * chunk_rows, spread_tile)
-        sent = sent.reshape(owners, chunk_rows, contrib.shape[0])
-        received.append(lax.all_to_all(sent, "grid", split_axis=0, concat_axis=0, tiled=True))
-
     half_ids = lax.iota(jnp.int32, half_cols)
-    panels, owns, others = [], [], []
-    for chunk in range(CHUNKS):
-        panel_part = place_columns(received[chunk], own_map, panel_ids, column_tile)
-        partner_part = swapped(panel_part, "cube", 0)
-        base = front_panel[chunk * chunk_rows : (chunk + 1) * chunk_rows]
-        panels.append(base + (panel_part.astype(jnp.float32) + partner_part.astype(jnp.float32)))
-        outgoing = place_columns(received[chunk], own_map, 2 * half_ids + other_index, column_tile)
-        others.append(swapped(outgoing, "cube", 0))
-        owns.append(place_columns(received[chunk], own_map, 2 * half_ids + half_index, column_tile))
-
-    top = jnp.zeros((PW, PW), jnp.float32)
-    for chunk in range(CHUNKS):
-        if chunk * chunk_rows < PW:
+    base_rows = [front_panel[c * chunk_rows : (c + 1) * chunk_rows] for c in range(CHUNKS)]
+    pivot_chunks = [chunk for chunk in range(CHUNKS) if chunk * chunk_rows < PW]
+    inverse_chunk = max(1, pivot_chunks[-1])
+    early_chunks = range(CHUNKS // 2)
+    sent, received, panels = {}, {}, {}
+    owns, others, inverse = {}, {}, None
+
+    def spread(chunk, after):
+        sent[chunk] = spread_rows(contrib, own_map, slot_rows + chunk * chunk_rows, spread_tile, after)
+        blocks = sent[chunk].reshape(owners, chunk_rows, contrib.shape[0])
+        received[chunk] = lax.all_to_all(blocks, "grid", split_axis=0, concat_axis=0, tiled=True)
+
+    def place(chunk, targets, after):
+        return place_columns(received[chunk], own_map, targets, column_tile, after)
+
+    row_ids = lax.iota(jnp.int32, chunk_rows)
+    row_pick = (2 * row_ids[: chunk_rows // 2, None] + half_index == row_ids[None, :]).astype(jnp.float32)
+
+    def parity_rows(panel, inverse):
+        return dot_exact(dot_exact(row_pick, panel), inverse, NT)
+
+    def inverse_of_pivot(after):
+        top = jnp.zeros((PW, PW), jnp.float32)
+        for chunk in pivot_chunks:
             start = grid_pos * owned_rows + chunk * chunk_rows
             inside = start < PW
             at = jnp.where(inside, start, 0)
             kept = lax.dynamic_slice_in_dim(top, at, chunk_rows, 0)
             top = lax.dynamic_update_slice_in_dim(top, jnp.where(inside, panels[chunk], kept), at, 0)
-    pivot_block = lax.psum(top, "grid")
-    inverse = inverse_factor(pivot_block)
+        return inverse_factor(lax.psum(top, "grid"), after)
+
+    spread(0, ())
+    spread(1, (sent[0],))
+    last, ready = sent[1], ()
+    for chunk in range(CHUNKS):
+        arrived = (others[chunk - 1],) if chunk else ()
+        wanted = arrived if chunk == CHUNKS - 1 else ready
+        panel_part = place(chunk, panel_ids, (last,) + wanted)
+        partner_part = swapped(panel_part, "cube", 0)
+        panels[chunk] = base_rows[chunk] + (panel_part.astype(jnp.float32) + partner_part.astype(jnp.float32))
+        outgoing = place(chunk, 2 * half_ids + other_index, (panel_part,))
+        others[chunk] = swapped(outgoing, "cube", 0)
+        last = outgoing
+        if chunk + 2 < CHUNKS:
+            owns[chunk] = place(chunk, 2 * half_ids + half_index, (outgoing,) + arrived)
+            spread(chunk + 2, (owns[chunk],))
+            last = sent[chunk + 2]
+        if chunk == inverse_chunk:
+            inverse = last = inverse_of_pivot((last,) + arrived)
+            early_rows = jnp.stack([parity_rows(panels[c], inverse) for c in early_chunks])
+            early = lax.all_gather(early_rows, "grid", axis=0, tiled=False)
+            ready = (early_rows,)
+        elif chunk == CHUNKS - 2:
+            last = owns[chunk] = place(chunk, 2 * half_ids + half_index, (outgoing,) + arrived)
+    owns[CHUNKS - 1] = place(CHUNKS - 1, 2 * half_ids + half_index, (outgoing,))
     half_inverse = dot_exact(own_pick, inverse)
 
-    row_ids = lax.iota(jnp.int32, chunk_rows)
-    row_pick = (2 * row_ids[: chunk_rows // 2, None] + half_index == row_ids[None, :]).astype(jnp.float32)
-    factors, halves, gathered = [], [], []
+    factors, halves = [], []
     for chunk in range(CHUNKS):
         factors.append(dot_exact(panels[chunk], inverse, NT))
         halves.append(dot_exact(panels[chunk], half_inverse, NT))
-        mine = dot_exact(row_pick, factors[chunk])
-        gathered.append(lax.all_gather(mine, "grid", axis=0, tiled=False))
-    columns = jnp.stack(gathered, axis=1).reshape(half_cols, PW)
+    late_rows = jnp.stack([parity_rows(panels[c], inverse) for c in range(CHUNKS // 2, CHUNKS)])
+    late = lax.all_gather(late_rows, "grid", axis=0, tiled=False)
+    columns = jnp.concatenate([early, late], axis=1).reshape(half_cols, PW)
 
     schur = None
     for chunk in range(CHUNKS):
@@ -274,7 +307,7 @@
             chunk, front, owns[chunk], others[chunk], factors[chunk], columns, schur, min(1024, half_cols)
         )
     panel_rows = jnp.concatenate(halves, axis=0)
-    return (schur[:, None, :], panel_rows[:, None, :])
+    return (schur.reshape(parent_front.shape), panel_rows[:, None, :])
 
 
 def solution(mesh):

time: 753 us -> 694 us (0.922)
  waiting for transfers between devices: 230 us -> 179 us
  local copies, waits for them, and re-layouts: 59.8 us -> 33.4 us
  matrix products: 27.8 us -> 40.4 us
    all_to_all x4, waiting for transfers between devices: 90.3 us -> 23.6 us  [spread(): lax.all_to_all(blocks, 'grid', split_axis=0, concat_axis=0, tiled=True)]
    unnamed x65 -> x40, local copies, waits for them, and re-layouts: 56 us -> 28.6 us
    ppermute x9, waiting for transfers between devices: 36.3 us -> 51.1 us  [swapped(): return lax.ppermute(block, axis, route)]
    dot_general x15 -> x19, matrix products: 16.7 us -> 29.5 us  [dot_exact(): lax.dot_general(left, right, dims, precision=HIGHEST, preferred_element_t...]
    concatenate x0 -> x1, other arithmetic: none -> 8.34 us  [shards(): columns = jnp.concatenate([early, late], axis=1).reshape(half_cols, PW)]
  transfers between devices with their start and end apart: 19 -> 17, of which waited for: 8 -> 7; matrix products, arithmetic and copies ran while one was open for 8% -> 11% of each run, Pallas kernels for 45% -> 48%
where the time goes in v2:
time: 694 us; the launch traced here: 688 us
  Pallas kernels  369 us (53%)
  waiting for transfers between devices  179 us (26%)
  matrix products  40.4 us (6%)
  local copies, waits for them, and re-layouts  33.4 us (5%)
  starting transfers between devices  30.5 us (4%)
  other arithmetic  21.2 us (3%)
  between operations  14.3 us (2%)
    pallas_call x12, Pallas kernels, place_columns(): pl.pallas_call(place_kernel, out_shape=jax.ShapeDtypeStruct((height, coun...  164 us
    pallas_call x4, Pallas kernels, spread_rows(): pl.pallas_call(functools.partial(spread_kernel, depth), out_shape=jax.Sha...  100 us
    all_gather x1, waiting for transfers between devices, shards(): lax.all_gather(child_panel, 'grid', axis=1, tiled=True)[0]  67.5 us
    pallas_call x1, Pallas kernels, inverse_factor(): pl.pallas_call(functools.partial(inverse_kernel, block), out_shape=jax.Sh...  61.3 us
    ppermute x9, waiting for transfers between devices, swapped(): return lax.ppermute(block, axis, route)  51.1 us
    pallas_call x4, Pallas kernels, update_rows(): pl.pallas_call(update_kernel, out_shape=jax.ShapeDtypeStruct((front.shape...  43.5 us
    psum x1, waiting for transfers between devices, inverse_of_pivot(): return inverse_factor(lax.psum(top, 'grid'), after)  35.6 us
    dot_general x19, matrix products, dot_exact(): lax.dot_general(left, right, dims, precision=HIGHEST, preferred_element_t...  29.5 us
  transfers between devices with their start and end apart: 17, of which 7 were waited for; matrix products, arithmetic and copies ran while one was open for 11% of the time, Pallas kernels for 48%

profile of v2, /device:TPU:0, one launch (start us, length us, event | category | flops | bytes accessed | tf_op | source)
XLA Modules:
  0.0 687.8 jit_solution(13647886907258163468)
XLA Ops:
  9.7 67.5 %all-gather.6.cloned.1.call-done = bf16[1,6144,512]{2,1,0:T(8,128)(2,1)} async-done(((bf16[1,768,512]{2,1,0:T(8,128)(2,1)}), bf16[1,6144,512]{2,1,0:T(8,128)(2,1)}) %all-gather.6.cloned.1.call-update) | async-done | bytes 6291472 | tf_op jit(solution)/shard_map/all_gather | solution.py:229
  77.1 10.9 %fusion.slab_ref = bf16[768,6144]{1,0:T(8,128)(2,1)} fusion(bf16[1,768,6144]{2,1,0:T(8,128)(2,1)} %param.5, bf16[1,6144,512]{2,1,0:T(8,128)(2,1)} %all-gather.6.cloned.1.call-done, bf16[1,768,512]{2,1,0:T(8,128)(2,1)} %param.6), kind=kOutput, calls=%fused_computation.1 | convolution fusion | flops 4845993984 | bytes 25952256 | tf_op jit(solution)/shard_map/ik,jk->ij/dot_general | solution.py:226
  88.1 25.1 %shard_map.59.rest_0_ = bf16[2048,768]{1,0:T(8,128)(2,1)} custom-call(s32[2048,1]{1,0:T(8,128)} %fusion.11.target_ref, s32[8,1,768]{2,1,0:T(1,128)} %bitcast.74, bf16[768,6144]{1,0:T(8,128)(2,1)} %fusion.slab_ref), custom_call_target="tpu_custom_call" | custom-call | flops 19327352832 | bytes 12582912 | tf_op jit(solution)/shard_map/pallas_call | solution.py:46
  117.8 19.1 %copy.21 = f32[1024,1,4096]{2,0,1:T(8,128)S(1)} copy(f32[1024,1,4096]{2,1,0:T(1,128)} %param.4) | data formatting | bytes 33554432
  136.9 5.8 copy-done.2
  151.9 25.1 %shard_map.60.rest_0_ = bf16[2048,768]{1,0:T(8,128)(2,1)} custom-call(s32[2048,1]{1,0:T(8,128)} %broadcast_add_fusion.2.target_ref, s32[8,1,768]{2,1,0:T(1,128)} %bitcast.75, bf16[768,6144]{1,0:T(8,128)(2,1)} %fusion.slab_ref, bf16[2048,768]{1,0:T(8,128)(2,1)} %shard_map.59.rest_0_), custom_call_target="tpu_custom_call" | custom-call | flops 19327352832 | bytes 12582912 | tf_op jit(solution)/shard_map/pallas_call | solution.py:46
  177.0 12.3 %all-to-all-done.1.rows_ref = bf16[8,256,768]{2,1,0:T(8,128)(2,1)} async-done(((bf16[8,256,768]{2,1,0:T(8,128)(2,1)}), bf16[8,256,768]{2,1,0:T(8,128)(2,1)}, u32[]{:S(2)}, u32[]{:S(2)}) %all-to-all-start.1) | async-done | bytes 3145760 | tf_op jit(solution)/shard_map/all_to_all | solution.py:249
  189.3 4.7 all-to-all-start
  206.3 18.1 %shard_map.62.rest_0_ = bf16[256,4096]{1,0:T(8,128)(2,1)} custom-call(s32[4096,1]{1,0:T(8,128)} %fusion.6.target_ref, s32[8,1,768]{2,1,0:T(1,128)} %bitcast.77, bf16[8,256,768]{2,1,0:T(8,128)(2,1)} %all-to-all-done.1.rows_ref, bf16[256,512]{1,0:T(8,128)(2,1)} %shard_map.61.rest_0_), custom_call_target="tpu_custom_call" | custom-call | flops 12884901888 | bytes 5242880 | tf_op jit(solution)/shard_map/pallas_call | solution.py:76
  225.0 18.1 %shard_map.63.rest_0_.own_ref = bf16[256,4096]{1,0:T(8,128)(2,1)} custom-call(s32[4096,1]{1,0:T(8,128)} %fusion.7.target_ref, s32[8,1,768]{2,1,0:T(1,128)} %bitcast.78, bf16[8,256,768]{2,1,0:T(8,128)(2,1)} %all-to-all-done.1.rows_ref, bf16[256,4096]{1,0:T(8,128)(2,1)} %shard_map.62.rest_0_), custom_call_target="tpu_custom_call" | custom-call | flops 12884901888 | bytes 5242880 | tf_op jit(solution)/shard_map/pallas_call | solution.py:76
  243.1 25.1 %shard_map.64.rest_0_ = bf16[2048,768]{1,0:T(8,128)(2,1)} custom-call(s32[2048,1]{1,0:T(8,128)} %broadcast_add_fusion.target_ref, s32[8,1,768]{2,1,0:T(1,128)} %bitcast.79, bf16[768,6144]{1,0:T(8,128)(2,1)} %fusion.slab_ref, bf16[256,4096]{1,0:T(8,128)(2,1)} %shard_map.63.rest_0_.own_ref), custom_call_target="tpu_custom_call" | custom-call | flops 19327352832 | bytes 12582912 | tf_op jit(solution)/shard_map/pallas_call | solution.py:46
  268.2 5.1 all-to-all-start.3
  274.0 4.6 shard_map.65.rest_0_
  280.1 18.1 %shard_map.66.rest_0_ = bf16[256,4096]{1,0:T(8,128)(2,1)} custom-call(s32[4096,1]{1,0:T(8,128)} %fusion.6.target_ref, s32[8,1,768]{2,1,0:T(1,128)} %bitcast.81, bf16[8,256,768]{2,1,0:T(8,128)(2,1)} %all-to-all-done.rows_ref, bf16[256,512]{1,0:T(8,128)(2,1)} %shard_map.65.rest_0_), custom_call_target="tpu_custom_call" | custom-call | flops 12884901888 | bytes 5242880 | tf_op jit(solution)/shard_map/pallas_call | solution.py:76
  304.0 18.5 %shard_map.67.rest_0_.own_ref = bf16[256,4096]{1,0:T(8,128)(2,1)} custom-call(s32[4096,1]{1,0:T(8,128)} %fusion.7.target_ref, s32[8,1,768]{2,1,0:T(1,128)} %bitcast.82, bf16[8,256,768]{2,1,0:T(8,128)(2,1)} %all-to-all-done.rows_ref, bf16[256,4096]{1,0:T(8,128)(2,1)} %shard_map.66.rest_0_, bf16[256,4096]{1,0:T(8,128)(2,1)} %collective-permute-done.rest_1_.other_ref), custom_call_target="tpu_custom_call" | custom-call | flops 12884901888 | bytes 5242880 | tf_op jit(solution)/shard_map/pallas_call | solution.py:76
  322.5 25.1 %shard_map.68.rest_0_ = bf16[2048,768]{1,0:T(8,128)(2,1)} custom-call(s32[2048,1]{1,0:T(8,128)} %broadcast_add_fusion.1.target_ref, s32[8,1,768]{2,1,0:T(1,128)} %bitcast.83, bf16[768,6144]{1,0:T(8,128)(2,1)} %fusion.slab_ref, bf16[256,4096]{1,0:T(8,128)(2,1)} %shard_map.67.rest_0_.own_ref), custom_call_target="tpu_custom_call" | custom-call | flops 19327352832 | bytes 12582912 | tf_op jit(solution)/shard_map/pallas_call | solution.py:46
  347.7 35.6 %all-reduce.2.cloned.1.call-done.pivot_ref = f32[512,512]{1,0:T(8,128)} async-done(((f32[512,512]{1,0:T(8,128)}), f32[512,512]{1,0:T(8,128)}) %all-reduce.2.cloned.1.call-update) | async-done | bytes 1048592 | tf_op jit(solution)/shard_map/psum | solution.py:268
  383.3 61.3 %shard_map.69.rest_0_ = f32[512,512]{1,0:T(8,128)} custom-call(f32[512,512]{1,0:T(8,128)} %all-reduce.2.cloned.1.call-done.pivot_ref, bf16[2048,768]{1,0:T(8,128)(2,1)} %shard_map.68.rest_0_, bf16[256,4096]{1,0:T(8,128)(2,1)} %collective-permute-done.rest_1_.other_ref), custom_call_target="tpu_custom_call" | custom-call | flops 40000000000 | bytes 2097152 | tf_op jit(solution)/shard_map/pallas_call | solution.py:139
  456.1 4.9 shard_map.70.rest_0_
  461.0 18.0 %shard_map.71.rest_0_ = bf16[256,4096]{1,0:T(8,128)(2,1)} custom-call(s32[4096,1]{1,0:T(8,128)} %fusion.6.target_ref, s32[8,1,768]{2,1,0:T(1,128)} %bitcast.85, bf16[8,256,768]{2,1,0:T(8,128)(2,1)} %all-to-all-done.3.rows_ref, bf16[256,512]{1,0:T(8,128)(2,1)} %shard_map.70.rest_0_), custom_call_target="tpu_custom_call" | custom-call | flops 12884901888 | bytes 5242880 | tf_op jit(solution)/shard_map/pallas_call | solution.py:76
  481.1 21.5 %collective-permute-done.4.rest_1_.other_ref = bf16[256,4096]{1,0:T(8,128)(2,1)S(1)} collective-permute-done((bf16[256,4096]{1,0:T(8,128)(2,1)}, bf16[256,4096]{1,0:T(8,128)(2,1)S(1)}, u32[]{:S(2)}, u32[]{:S(2)}) %collective-permute-start.4) | collective-permute-done | bytes 2097184 | tf_op jit(solution)/shard_map/ppermute | solution.py:25
  503.9 18.1 %shard_map.72.rest_0_.own_ref = bf16[256,4096]{1,0:T(8,128)(2,1)} custom-call(s32[4096,1]{1,0:T(8,128)} %fusion.7.target_ref, s32[8,1,768]{2,1,0:T(1,128)} %bitcast.86, bf16[8,256,768]{2,1,0:T(8,128)(2,1)} %all-to-all-done.3.rows_ref, bf16[256,4096]{1,0:T(8,128)(2,1)} %shard_map.71.rest_0_, bf16[256,4096]{1,0:T(8,128)(2,1)} %copy-done.13), custom_call_target="tpu_custom_call" | custom-call | flops 12884901888 | bytes 5242880 | tf_op jit(solution)/shard_map/pallas_call | solution.py:76
  522.0 25.6 %collective-permute-done.5.rest_1_.other_ref = bf16[256,4096]{1,0:T(8,128)(2,1)} collective-permute-done((bf16[256,4096]{1,0:T(8,128)(2,1)}, bf16[256,4096]{1,0:T(8,128)(2,1)}, u32[]{:S(2)}, u32[]{:S(2)}) %collective-permute-start.5) | collective-permute-done | bytes 2097184 | tf_op jit(solution)/shard_map/ppermute | solution.py:25
  547.6 11.3 %all-to-all-done.2.rows_ref = bf16[8,256,768]{2,1,0:T(8,128)(2,1)} async-done(((bf16[8,256,768]{2,1,0:T(8,128)(2,1)}), bf16[8,256,768]{2,1,0:T(8,128)(2,1)}, u32[]{:S(2)}, u32[]{:S(2)}) %all-to-all-start.2) | async-done | bytes 3145760 | tf_op jit(solution)/shard_map/all_to_all | solution.py:249
  559.6 4.7 shard_map.73.rest_0_
  586.6 18.1 %shard_map.74.rest_0_ = bf16[256,4096]{1,0:T(8,128)(2,1)} custom-call(s32[4096,1]{1,0:T(8,128)} %fusion.6.target_ref, s32[8,1,768]{2,1,0:T(1,128)} %bitcast.88, bf16[8,256,768]{2,1,0:T(8,128)(2,1)} %all-to-all-done.2.rows_ref, bf16[256,512]{1,0:T(8,128)(2,1)} %shard_map.73.rest_0_), custom_call_target="tpu_custom_call" | custom-call | flops 12884901888 | bytes 5242880 | tf_op jit(solution)/shard_map/pallas_call | solution.py:76
  606.1 18.4 %shard_map.75.own_ref = bf16[256,4096]{1,0:T(8,128)(2,1)} custom-call(s32[4096,1]{1,0:T(8,128)} %fusion.7.target_ref, s32[8,1,768]{2,1,0:T(1,128)} %bitcast.89, bf16[8,256,768]{2,1,0:T(8,128)(2,1)} %all-to-all-done.2.rows_ref, bf16[256,4096]{1,0:T(8,128)(2,1)} %shard_map.74.rest_0_), custom_call_target="tpu_custom_call" | custom-call | flops 12884901888 | bytes 5242880 | tf_op jit(solution)/shard_map/pallas_call | solution.py:76
  629.2 8.3 %pad_maximum_fusion = f32[8,4,128,512]{3,2,1,0:T(8,128)} fusion(f32[8,2,128,512]{3,2,1,0:T(8,128)} %bitcast.71, f32[8,2,128,512]{3,2,1,0:T(8,128)} %bitcast.70), kind=kLoop, calls=%fused_computation.3 | loop fusion | flops 2097152 | bytes 16777216 | tf_op jit(solution)/shard_map/concatenate | solution.py:302
  637.5 10.9 %shard_map.76.rest_0_ = f32[1024,32,128]{2,1,0:T(8,128)} custom-call(f32[1024,4096]{1,0:T(8,128)} %bitcast.59, bf16[256,4096]{1,0:T(8,128)(2,1)} %shard_map.63.rest_0_.own_ref, bf16[256,4096]{1,0:T(8,128)(2,1)} %collective-permute-done.rest_1_.other_ref, f32[256,512]{1,0:T(8,128)} %fusion.35.factor_ref, f32[4096,512]{1,0:T(8,128)} %bitcast.64), custom_call_target="tpu_custom_call" | custom-call | flops 3221225472 | bytes 20971520 | tf_op jit(solution)/shard_map/pallas_call | solution.py:192
  648.4 10.9 %shard_map.77.rest_0_ = f32[1024,32,128]{2,1,0:T(8,128)} custom-call(f32[1024,4096]{1,0:T(8,128)} %bitcast.60, bf16[256,4096]{1,0:T(8,128)(2,1)} %shard_map.67.rest_0_.own_ref, bf16[256,4096]{1,0:T(8,128)(2,1)} %copy-done.13, f32[256,512]{1,0:T(8,128)} %fusion.34.factor_ref, f32[4096,512]{1,0:T(8,128)} %bitcast.65, ...), custom_call_target="tpu_custom_call", output_to_operand_aliasing={{}: (5, {})} | custom-call | flops 3221225472 | bytes 20971520 | tf_op jit(solution)/shard_map/pallas_call | solution.py:192
  659.3 10.9 %shard_map.78.rest_0_ = f32[1024,32,128]{2,1,0:T(8,128)} custom-call(f32[1024,4096]{1,0:T(8,128)} %bitcast.61, bf16[256,4096]{1,0:T(8,128)(2,1)} %shard_map.72.rest_0_.own_ref, bf16[256,4096]{1,0:T(8,128)(2,1)} %collective-permute-done.5.rest_1_.other_ref, f32[256,512]{1,0:T(8,128)} %fusion.33.factor_ref, ...), custom_call_target="tpu_custom_call", output_to_operand_aliasing={{}: (5, {})} | custom-call | flops 3221225472 | bytes 20971520 | tf_op jit(solution)/shard_map/pallas_call | solution.py:192
  670.2 10.9 %shard_map.79 = f32[1024,32,128]{2,1,0:T(8,128)} custom-call(f32[1024,4096]{1,0:T(8,128)} %bitcast.62, bf16[256,4096]{1,0:T(8,128)(2,1)} %shard_map.75.own_ref, bf16[256,4096]{1,0:T(8,128)(2,1)} %collective-permute-done.6.other_ref, f32[256,512]{1,0:T(8,128)} %fusion.31.factor_ref, f32[4096,512]{1,0:T(8,128)} %bitcast.67, ...), custom_call_target="tpu_custom_call", output_to_operand_aliasing={{}: (5, {})} | custom-call | flops 3221225472 | bytes 20971520 | tf_op jit(solution)/shard_map/pallas_call | solution.py:192
  (110 shorter events, 81.0 us)
Async XLA Ops:
  7.2 70.0 %all-gather.6.cloned.1.call-start = ((), (), s32[]{:S(2)}) async-start(), calls=%async_computation.4 | async-start | bytes 7077888 | tf_op jit(solution)/shard_map/all_gather | solution.py:229
  113.2 76.1 %all-to-all-start.1 = ((bf16[8,256,768]{2,1,0:T(8,128)(2,1)}), bf16[8,256,768]{2,1,0:T(8,128)(2,1)}, u32[]{:S(2)}, u32[]{:S(2)}) async-start(bf16[8,256,768]{2,1,0:T(8,128)(2,1)} %bitcast.73), calls=%async_computation.1 | async-start | bytes 6291456 | tf_op jit(solution)/shard_map/all_to_all | solution.py:249
  136.9 5.8 copy-start.2
  142.8 54.0 %collective-permute-start.1 = (f32[1024,256]{1,0:T(8,128)S(1)}, f32[1024,256]{1,0:T(8,128)S(1)}, u32[]{:S(2)}, u32[]{:S(2)}) collective-permute-start(f32[1024,256]{1,0:T(8,128)S(1)} %slice.24), channel_id=1, source_target_pairs={{0,8},{8,0},{16,24},{24,16},{1,9},{9,1},{17,25},{25,17},{2,10},{10... | collective-permute-start | bytes 3145736 | tf_op jit(solution)/shard_map/ppermute | solution.py:25
  144.3 6.0 copy-start.17
  189.3 78.9 %all-to-all-start = ((bf16[8,256,768]{2,1,0:T(8,128)(2,1)}), bf16[8,256,768]{2,1,0:T(8,128)(2,1)}, u32[]{:S(2)}, u32[]{:S(2)}) async-start(bf16[8,256,768]{2,1,0:T(8,128)(2,1)} %bitcast.69), calls=%async_computation | async-start | bytes 6291456 | tf_op jit(solution)/shard_map/all_to_all | solution.py:249
  204.9 93.3 %collective-permute-start.2 = (bf16[256,512]{1,0:T(8,128)(2,1)}, bf16[256,512]{1,0:T(8,128)(2,1)S(1)}, u32[]{:S(2)}, u32[]{:S(2)}) collective-permute-start(bf16[256,512]{1,0:T(8,128)(2,1)} %shard_map.61.rest_0_), channel_id=1, source_target_pairs={{0,8},{8,0},{16,24},{24,16},{1,9},{9,1},{17,25},{25,17},{2,10},{10... | collective-permute-start | bytes 786440 | tf_op jit(solution)/shard_map/ppermute | solution.py:25
  224.4 79.6 %collective-permute-start = (bf16[256,4096]{1,0:T(8,128)(2,1)}, bf16[256,4096]{1,0:T(8,128)(2,1)}, u32[]{:S(2)}, u32[]{:S(2)}) collective-permute-start(bf16[256,4096]{1,0:T(8,128)(2,1)} %shard_map.62.rest_0_), channel_id=1, source_target_pairs={{0,8},{8,0},{16,24},{24,16},{1,9},{9,1},{17,25},{25,17},{2,10},{10... | collective-permute-start | bytes 6291464 | tf_op jit(solution)/shard_map/ppermute | solution.py:25
  268.2 181.0 %all-to-all-start.3 = ((bf16[8,256,768]{2,1,0:T(8,128)(2,1)}), bf16[8,256,768]{2,1,0:T(8,128)(2,1)}, u32[]{:S(2)}, u32[]{:S(2)}) async-start(bf16[8,256,768]{2,1,0:T(8,128)(2,1)} %bitcast.68), calls=%async_computation.3 | async-start | bytes 6291456 | tf_op jit(solution)/shard_map/all_to_all | solution.py:249
  273.3 110.0 %all-reduce.2.cloned.1.call-start = ((), (), s32[]{:S(2)}) async-start(), calls=%async_computation.5 | async-start | bytes 2097152 | tf_op jit(solution)/shard_map/psum | solution.py:268
  278.7 20.7 %copy-start.16 = (bf16[256,512]{1,0:T(8,128)(2,1)S(1)}, bf16[256,512]{1,0:T(8,128)(2,1)}, u32[]{:S(2)}) copy-start(bf16[256,512]{1,0:T(8,128)(2,1)} %shard_map.61.rest_0_) | copy-start | bytes 786436
  278.7 21.6 %collective-permute-start.3 = (bf16[256,512]{1,0:T(8,128)(2,1)}, bf16[256,512]{1,0:T(8,128)(2,1)S(1)}, u32[]{:S(2)}, u32[]{:S(2)}) collective-permute-start(bf16[256,512]{1,0:T(8,128)(2,1)} %shard_map.65.rest_0_), channel_id=1, source_target_pairs={{0,8},{8,0},{16,24},{24,16},{1,9},{9,1},{17,25},{25,17},{2,10},{10... | collective-permute-start | bytes 786440 | tf_op jit(solution)/shard_map/ppermute | solution.py:25
  300.3 2.7 copy-start.7
  302.5 20.0 %copy-start.5 = (f32[256,512]{1,0:T(8,128)}, f32[256,512]{1,0:T(8,128)S(1)}, u32[]{:S(2)}) copy-start(f32[256,512]{1,0:T(8,128)S(1)} %get-tuple-element.7) | copy-start | bytes 1572868
  302.6 326.6 %all-gather.8.cloned.1.call-start = ((), (), s32[]{:S(2)}) async-start(), calls=%async_computation.6 | async-start | bytes 4718592 | tf_op jit(solution)/shard_map/all_gather | solution.py:289
  347.7 99.4 %copy-start.14 = (f32[128,512]{1,0:T(8,128)S(1)}, f32[128,512]{1,0:T(8,128)}, u32[]{:S(2)}) copy-start(f32[128,512]{1,0:T(8,128)} %fusion.22) | copy-start | bytes 786436
  444.6 2.5 copy-start.3
  449.2 109.7 %all-to-all-start.2 = ((bf16[8,256,768]{2,1,0:T(8,128)(2,1)}), bf16[8,256,768]{2,1,0:T(8,128)(2,1)}, u32[]{:S(2)}, u32[]{:S(2)}) async-start(bf16[8,256,768]{2,1,0:T(8,128)(2,1)} %bitcast.72), calls=%async_computation.2 | async-start | bytes 6291456 | tf_op jit(solution)/shard_map/all_to_all | solution.py:249
  453.6 175.5 %all-gather.10.cloned.1.call-start = ((), (), s32[]{:S(2)}) async-start(), calls=%async_computation.7 | async-start | bytes 4718592 | tf_op jit(solution)/shard_map/all_gather | solution.py:301
  453.9 48.7 %collective-permute-start.4 = (bf16[256,4096]{1,0:T(8,128)(2,1)}, bf16[256,4096]{1,0:T(8,128)(2,1)S(1)}, u32[]{:S(2)}, u32[]{:S(2)}) collective-permute-start(bf16[256,4096]{1,0:T(8,128)(2,1)} %shard_map.66.rest_0_), channel_id=1, source_target_pairs={{0,8},{8,0},{16,24},{24,16},{1,9},{9,1},{17,25},{25,17},{2,10},{10... | collective-permute-start | bytes 6291464 | tf_op jit(solution)/shard_map/ppermute | solution.py:25
  479.0 68.6 %collective-permute-start.5 = (bf16[256,4096]{1,0:T(8,128)(2,1)}, bf16[256,4096]{1,0:T(8,128)(2,1)}, u32[]{:S(2)}, u32[]{:S(2)}) collective-permute-start(bf16[256,4096]{1,0:T(8,128)(2,1)} %shard_map.71.rest_0_), channel_id=1, source_target_pairs={{0,8},{8,0},{16,24},{24,16},{1,9},{9,1},{17,25},{25,17},{2,10},{10... | collective-permute-start | bytes 6291464 | tf_op jit(solution)/shard_map/ppermute | solution.py:25
  479.5 86.3 %collective-permute-start.8 = (bf16[256,512]{1,0:T(8,128)(2,1)}, bf16[256,512]{1,0:T(8,128)(2,1)}, u32[]{:S(2)}, u32[]{:S(2)}) collective-permute-start(bf16[256,512]{1,0:T(8,128)(2,1)} %shard_map.70.rest_0_), channel_id=1, source_target_pairs={{0,8},{8,0},{16,24},{24,16},{1,9},{9,1},{17,25},{25,17},{2,10},{10... | collective-permute-start | bytes 786440 | tf_op jit(solution)/shard_map/ppermute | solution.py:25
  559.6 7.6 %copy-start.4 = (f32[512,512]{1,0:T(8,128)S(1)}, f32[512,512]{1,0:T(8,128)}, u32[]{:S(2)}) copy-start(f32[512,512]{1,0:T(8,128)} %shard_map.69.rest_0_) | copy-start | bytes 3145732
  564.3 8.1 %copy-start.9 = (bf16[256,512]{1,0:T(8,128)(2,1)S(1)}, bf16[256,512]{1,0:T(8,128)(2,1)}, u32[]{:S(2)}) copy-start(bf16[256,512]{1,0:T(8,128)(2,1)} %shard_map.73.rest_0_) | copy-start | bytes 786436
  564.3 8.1 %collective-permute-start.7 = (bf16[256,512]{1,0:T(8,128)(2,1)}, bf16[256,512]{1,0:T(8,128)(2,1)S(1)}, u32[]{:S(2)}, u32[]{:S(2)}) collective-permute-start(bf16[256,512]{1,0:T(8,128)(2,1)} %shard_map.73.rest_0_), channel_id=1, source_target_pairs={{0,8},{8,0},{16,24},{24,16},{1,9},{9,1},{17,25},{25,17},{2,10},{10... | collective-permute-start | bytes 786440 | tf_op jit(solution)/shard_map/ppermute | solution.py:25
  568.4 6.7 copy-start.18
  575.1 2.4 copy-start.8
  575.1 3.0 copy-start.6
  604.6 19.8 %copy-start.10 = (bf16[256,512]{1,0:T(8,128)(2,1)S(1)}, bf16[256,512]{1,0:T(8,128)(2,1)}, u32[]{:S(2)}) copy-start(bf16[256,512]{1,0:T(8,128)(2,1)} %shard_map.73.rest_0_) | copy-start | bytes 786436
  604.6 19.8 %copy-start.12 = (bf16[256,512]{1,0:T(8,128)(2,1)S(1)}, bf16[256,512]{1,0:T(8,128)(2,1)}, u32[]{:S(2)}) copy-start(bf16[256,512]{1,0:T(8,128)(2,1)} %copy-done.11) | copy-start | bytes 786436
  604.6 65.5 %collective-permute-start.6 = (bf16[256,4096]{1,0:T(8,128)(2,1)}, bf16[256,4096]{1,0:T(8,128)(2,1)}, u32[]{:S(2)}, u32[]{:S(2)}) collective-permute-start(bf16[256,4096]{1,0:T(8,128)(2,1)} %shard_map.74.rest_0_), channel_id=1, source_target_pairs={{0,8},{8,0},{16,24},{24,16},{1,9},{9,1},{17,25},{25,17},{2,10},{10... | collective-permute-start | bytes 6291464 | tf_op jit(solution)/shard_map/ppermute | solution.py:25
  670.1 10.9 %copy-start.1 = (s32[4,6144]{1,0:T(4,128)S(1)}, s32[4,6144]{1,0:T(4,128)}, u32[]{:S(2)}) copy-start(s32[4,6144]{1,0:T(4,128)} %param.7) | copy-start | bytes 294916
  (4 other events, 6.1 us)
Sparse Core Ops, SparseCore 0:
  9.7 67.4 all-gather.5
  302.7 80.5 all-reduce.1
  449.3 95.6 all-gather.7
  575.2 46.3 all-gather.9
